TPU v7x, 32 devices: a whole 2x2x4 slice. The times are simulated.
32 devices in a mesh: dp: 8 (over z, y), group: 4 (over x, core).
Axes of the slice: x: 2, y: 2, z: 4, core: 2. Of those that a mesh axis runs over, the one named last changes fastest.
Arguments:
- features: bfloat16 [2, 32, 128, 512], P(None, ('dp', 'group')), may hold values from -6 to 6
- span_starts: int32 [2, 32, 10], P(None, ('dp', 'group')), may hold values from 0 to 128, as said below
- labels: int32 [2, 32, 128], P(None, ('dp', 'group')), may hold values from 0 to 503
- feature_norm: float32 [2, 512], replicated
- feature_first: float32 [2, 512], replicated, may hold values from -1.9073486e-05 to 1.9073486e-05
- feature_second: float32 [2, 512], replicated, may hold values from 2.6034745e-12 to 1.0381954e-11
- projection: float32 [512, 768], P('dp', 'group'), may hold values from -0.25 to 0.25
- projection_first: float32 [512, 768], P('dp', 'group'), may hold values from -4.7683716e-06 to 4.7683716e-06
- projection_second: float32 [512, 768], P('dp', 'group'), may hold values from 1.6291681e-13 to 6.5166725e-13
- vectors: float32 [7, 768], replicated
- vector_first: float32 [7, 768], replicated, may hold values from -1.9073486e-05 to 1.9073486e-05
- vector_second: float32 [7, 768], replicated, may hold values from 2.6034745e-12 to 1.0381954e-11
- conv_weight: float32 [128, 48, 768], P('group', None, 'dp'), may hold values from -0.078125 to 0.078125
- conv_first: float32 [128, 48, 768], P('group', None, 'dp'), may hold values from -4.7683716e-06 to 4.7683716e-06
- conv_second: float32 [128, 48, 768], P('group', None, 'dp'), may hold values from 1.6291681e-13 to 6.5166725e-13
- head: float32 [768, 256], P('dp', 'group'), may hold values from -0.21875 to 0.21875
- head_first: float32 [768, 256], P('dp', 'group'), may hold values from -4.7683716e-06 to 4.7683716e-06
- head_second: float32 [768, 256], P('dp', 'group'), may hold values from 1.6291681e-13 to 6.5166725e-13
- clusters: float32 [504, 256], P('group', 'dp'), may hold values from -0.3 to 0.3
- cluster_first: float32 [504, 256], P('group', 'dp'), may hold values from -4.7683716e-06 to 4.7683716e-06
- cluster_second: float32 [504, 256], P('group', 'dp'), may hold values from 1.6291681e-13 to 6.5166725e-13
- blocks: float32 [12, 768, 768], P('group', 'dp'), may hold values from -0.21875 to 0.21875
- statistics: float32 [12, 2, 768, 768], P('group', None, 'dp'), as said below
Outputs:
- loss_sum: float32 [], replicated
- masked_count: float32 [], replicated
- grad_norm: float32 [], replicated
- feature_first_new: float32 [2, 512], replicated
- feature_second_new: float32 [2, 512], replicated
- feature_norm_new: float32 [2, 512], replicated
- projection_first_new: float32 [512, 768], P('dp', 'group')
- projection_second_new: float32 [512, 768], P('dp', 'group')
- projection_new: float32 [512, 768], P('dp', 'group')
- vector_first_new: float32 [7, 768], replicated
- vector_second_new: float32 [7, 768], replicated
- vectors_new: float32 [7, 768], replicated
- conv_first_new: float32 [128, 48, 768], P('group', None, 'dp')
- conv_second_new: float32 [128, 48, 768], P('group', None, 'dp')
- conv_weight_new: float32 [128, 48, 768], P('group', None, 'dp')
- head_first_new: float32 [768, 256], P('dp', 'group')
- head_second_new: float32 [768, 256], P('dp', 'group')
- head_new: float32 [768, 256], P('dp', 'group')
- cluster_first_new: float32 [504, 256], P('group', 'dp')
- cluster_second_new: float32 [504, 256], P('group', 'dp')
- clusters_new: float32 [504, 256], P('group', 'dp')
- block_grad: float32 [12, 768, 768], P('group', 'dp')
- statistics_new: float32 [12, 2, 768, 768], P('group', None, 'dp')
- blocks_new: float32 [12, 768, 768], P('group', 'dp')
Inputs may be any that keep to these rules, and one draw needn't show every extreme that they name: `span_starts`: an entry equal to 128 names no span; every other entry is at most 118; every clip has at least 3 spans. `statistics`: each left and right matrix is symmetric and positive definite.
All inputs are finite; a program needn't handle non-finite values.
Results may differ from a plain program's by a relative error of at most 0.008.
The roundings to bfloat16 on the way count: a program that leaves them out, or rounds other values in their place, can miss the bound.
Values may be sent and summed in bfloat16 or wider, within the bound.
A program may use at most 448 MiB of HBM per device.

v0:
```python
import functools

import jax
import jax.numpy as jnp
from jax import lax
from jax.experimental import pallas as pl
from jax.experimental.pallas import tpu as pltpu
from jax.sharding import PartitionSpec as P

D = 768
HEADS = 12
HEAD = 64
TAPS = 128
CLIP = 128
SPAN = 10
NEWTON = 3
STEP = 10


HIGH = lax.Precision.HIGHEST
beta_one = 0.9
beta_two = 0.98
adam_eps = 1e-08
rate_matrix = 0.02
rate_vector = 0.5
rate_shampoo = 0.2
decay_weight = 0.01
stat_decay = 0.95
max_norm = 0.01
inv_temp = 10.0
STRIDE = 4


def for_sending(array):

    def short(part):
        return part.astype(jnp.bfloat16) if part.dtype == jnp.float32 else part

    return jax.tree.map(short, array)


def spread_2(array, axis, root):
    mine = lax.axis_index(axis) == root
    return lax.psum(jnp.where(mine, array, jnp.zeros_like(array)), axis)


def to_low(values):
    return values.astype(jnp.bfloat16)


def frame_mask(starts):
    frames = jnp.arange(CLIP, dtype=jnp.int32)[:, None]
    inside = (frames >= starts[None, :]) & (frames < starts[None, :] + SPAN)
    return jnp.any(inside, axis=1).astype(jnp.float32)


def inverse_root(matrix):
    size = matrix.shape[0]
    identity = jnp.eye(size, dtype=jnp.float32)
    damped = matrix + 0.0001 * (jnp.trace(matrix) / size) * identity
    magnitude = jnp.sqrt(jnp.sum(damped * damped))
    current = damped / magnitude
    result = identity * magnitude ** (-0.25)
    for sweep in range(NEWTON):
        factor = (5.0 * identity - current) * 0.25
        result = jnp.dot(result, factor, precision=HIGH)
        square = jnp.dot(factor, factor, precision=HIGH)
        current = jnp.dot(jnp.dot(square, square, precision=HIGH), current, precision=HIGH)
    return result


def adamw(weight, grad, first, second, rate, decay):
    first = beta_one * first + (1 - beta_one) * grad
    second = beta_two * second + (1 - beta_two) * grad * grad
    corrected = first / (1 - beta_one**STEP)
    scaled = jnp.sqrt(second / (1 - beta_two**STEP)) + adam_eps
    return (first, second, weight - rate * (corrected / scaled + decay * weight))


def reduce_grads(parts):
    proj_part, kernel_part, head_part, center_part, block_part = parts
    grouped = (
        lax.psum_scatter(proj_part, "group", scatter_dimension=1, tiled=True),
        lax.psum_scatter(kernel_part, "group", scatter_dimension=0, tiled=True),
        lax.psum_scatter(head_part, "group", scatter_dimension=1, tiled=True),
        lax.psum_scatter(center_part, "group", scatter_dimension=0, tiled=True),
        lax.psum_scatter(block_part, "group", scatter_dimension=0, tiled=True),
    )
    proj_part, kernel_part, head_part, center_part, block_part = grouped
    return (
        lax.psum_scatter(proj_part, "dp", scatter_dimension=0, tiled=True),
        lax.psum_scatter(kernel_part, "dp", scatter_dimension=2, tiled=True),
        lax.psum_scatter(head_part, "dp", scatter_dimension=0, tiled=True),
        lax.psum_scatter(center_part, "dp", scatter_dimension=1, tiled=True),
        lax.psum_scatter(block_part, "dp", scatter_dimension=1, tiled=True),
    )


def gather_plain(projection, conv_weight, head, clusters, blocks):
    gathered = (
        lax.all_gather(to_low(projection), "dp", axis=0, tiled=True),
        lax.all_gather(to_low(conv_weight), "dp", axis=2, tiled=True),
        lax.all_gather(to_low(head), "dp", axis=0, tiled=True),
        lax.all_gather(to_low(clusters), "dp", axis=1, tiled=True),
        lax.all_gather(to_low(blocks), "dp", axis=1, tiled=True),
    )
    proj_part, kernel_part, head_part, center_part, block_part = gathered
    return (
        lax.all_gather(proj_part, "group", axis=1, tiled=True),
        lax.all_gather(kernel_part, "group", axis=0, tiled=True),
        lax.all_gather(head_part, "group", axis=1, tiled=True),
        lax.all_gather(center_part, "group", axis=0, tiled=True),
        lax.all_gather(block_part, "group", axis=0, tiled=True),
    )


def shampoo_plain(block_rows, statistics):
    full_blocks = lax.all_gather(block_rows.astype(jnp.bfloat16), "dp", axis=1, tiled=True).astype(
        block_rows.dtype
    )
    rows = block_rows.shape[1]
    here = lax.axis_index("dp")
    first_row = here * rows
    column_slice = lax.dynamic_slice_in_dim(full_blocks, first_row, rows, 2)
    left_rows = stat_decay * statistics[:, 0] + (1 - stat_decay) * jnp.einsum(
        "brk,bck->brc", block_rows, full_blocks, precision=HIGH
    )
    right_rows = stat_decay * statistics[:, 1] + (1 - stat_decay) * jnp.einsum(
        "bkr,bkc->brc", column_slice, full_blocks, precision=HIGH
    )
    group_blocks = block_rows.shape[0]
    dp_size = lax.axis_size("dp")
    owners = [
        (2 * member + side) * dp_size // (2 * group_blocks)
        for member in range(group_blocks)
        for side in range(2)
    ]
    left_full, right_full = (
        lax.all_gather(left_rows.astype(jnp.bfloat16), "dp", axis=1, tiled=True).astype(
            left_rows.dtype
        ),
        lax.all_gather(right_rows.astype(jnp.bfloat16), "dp", axis=1, tiled=True).astype(
            right_rows.dtype
        ),
    )
    sources = [
        left_full[member] if side == 0 else right_full[member]
        for member in range(group_blocks)
        for side in range(2)
    ]
    roots = []
    for index in range(2 * group_blocks):
        owner = owners[index]
        root = lax.cond(here == owner, inverse_root, jnp.zeros_like, sources[index])
        root = spread_2(for_sending(root), "dp", owner).astype(root.dtype)
        roots.append(root)
    stacked = jnp.stack(roots).reshape(group_blocks, 2, D, D)
    left_root_rows = lax.dynamic_slice_in_dim(stacked[:, 0], first_row, rows, 1)
    update_rows = jnp.einsum(
        "brk,bkc->brc",
        jnp.einsum("brk,bkc->brc", left_root_rows, full_blocks, precision=HIGH),
        stacked[:, 1],
        precision=HIGH,
    )
    return jnp.stack([left_rows, right_rows], 1), update_rows


MESH = pl.DeviceIdType.MESH
HBM = pl.BlockSpec(memory_space=pltpu.HBM)
VMEM = pl.BlockSpec(memory_space=pltpu.VMEM)
VMEM_LIMIT = 60 * 1024 * 1024


class Place:
    def __init__(self, dp_size, group_size):
        self.dp_size, self.group_size = dp_size, group_size
        self.lines = dp_size // 2
        self.dp, self.group = lax.axis_index("dp"), lax.axis_index("group")
        self.z, self.y = self.dp // 2, self.dp % 2
        self.x, self.core = self.group // 2, self.group % 2

    def at(self, z, flip_y=0, flip_x=0, flip_core=0):
        y = self.y + flip_y * (1 - 2 * self.y)
        x = self.x + flip_x * (1 - 2 * self.x)
        core = self.core + flip_core * (1 - 2 * self.core)
        return (z * 2 + y, x * 2 + core)

    def near(self, z, p, q):
        return self.at(z, p * (1 - self.core) + q * self.core, q * (1 - self.core) + p * self.core)

    def across(self, z, p, q):
        return self.at(z, p * self.core + q * (1 - self.core), q * self.core + p * (1 - self.core), 1)


def greet(place):
    barrier = pltpu.get_barrier_semaphore()
    first = place.x * 2
    for other in range(place.dp_size):
        for core in range(2):

            @pl.when((place.dp != other) | (place.core != core))
            def _():
                pl.semaphore_signal(
                    barrier, inc=1, device_id=(other, first + core), device_id_type=MESH
                )

    for core in range(2):
        pl.semaphore_signal(
            barrier,
            inc=1,
            device_id=(place.dp, (1 - place.x) * 2 + core),
            device_id_type=MESH,
        )
    pl.semaphore_wait(barrier, 2 * place.dp_size - 1 + 2)


def guarded(condition, action):
    if condition is None:
        action()
    else:
        pl.when(condition)(action)


def both(one, two):
    if one is None:
        return two
    if two is None:
        return one
    return one & two


def piece_at(kind, ref, dp, group, shape):
    if kind == "blocks":
        start = pl.multiple_of(dp * shape[1], shape[1])
        return ref.at[pl.ds(group * shape[0], shape[0]), pl.ds(start, shape[1])]
    if kind == "conv":
        return ref.at[group, pl.ds(dp * shape[0], shape[0])]
    return ref.at[dp, group]


KINDS = ("conv", "small", "blocks")


def make_shards(refs, mask, conv, small, blocks_low, stats_low):
    starts, projection, weight, head_t, clusters_t, blocks, statistics = refs
    for clip in range(starts.shape[0]):
        frame = lax.broadcasted_iota(jnp.int32, (CLIP, starts.shape[1]), 0)
        begins = starts[clip : clip + 1, :]
        inside = ((frame >= begins) & (frame < begins + SPAN)).astype(jnp.float32)
        mask[clip * CLIP : (clip + 1) * CLIP, :] = jnp.max(inside, 1, keepdims=True)
    note = jnp.sum(mask[...], 0, keepdims=True)
    runs, steps, c, channels = weight.shape
    for offset in range(steps):
        turned = weight[:, offset].reshape(runs * c, channels).T.astype(jnp.bfloat16)
        for group in range(channels // c):
            conv[group, offset * c : (offset + 1) * c, :] = turned[group * c : (group + 1) * c]
    low = jnp.bfloat16

    def padded(values):
        spare = jnp.zeros((values.shape[0], 128 - values.shape[1]), jnp.float32)
        return jnp.concatenate([values, spare], 1)

    small[0:64, :] = projection[:, 0:128].astype(low)
    small[64:128, :] = padded(projection[:, 128:]).astype(low)
    small[128:224, :] = padded(head_t[...].T).astype(low)
    lane = lax.broadcasted_iota(jnp.int32, (32, 128), 1)
    small[224:256, :] = jnp.where(lane < CLUSTER_ROWS, padded(clusters_t[...]), note).astype(low)
    blocks_low[...] = blocks[...].astype(low)
    stats_low[...] = statistics[...].astype(low)


def gather_kernel(sizes, shapes, taps, *refs):
    place = Place(*sizes)
    count = len(KINDS)
    refs = list(refs)

    def pull(number):
        taken = refs[:number]
        del refs[:number]
        return taken

    raw, (features, feature_norm, vectors) = pull(7), pull(3)
    outs, results, (mask, stats_low) = pull(count), pull(7), pull(2)
    ins, (small_here,), scratch = pull(count), pull(1), pull(5)
    (send_sem, recv_sem, own_sem, small_sem) = pull(4)
    z, last = place.z, place.lines - 1
    me = (place.dp, place.group)
    make_shards(raw, mask, *ins, stats_low)
    greet(place)
    sent = []
    slots = [0] * count
    conv, tiny = KINDS.index("conv"), KINDS.index("small")
    enter, project, convolve, leave = front_compute(
        taps,
        (features, mask, feature_norm, vectors, small_here, outs[conv]),
        results,
        scratch,
    )

    def view(k, source):
        return piece_at(KINDS[k], outs[k], source[0], source[1], shapes[k])

    def identity(source):
        return source[0] * place.group_size + source[1]

    def copy_of(k, source, target, slot, own=False):
        spot = view(k, source)
        return pltpu.make_async_remote_copy(
            src_ref=ins[k] if own else spot,
            dst_ref=spot,
            send_sem=send_sem.at[k, slot],
            recv_sem=recv_sem.at[k, identity(source)],
            device_id=target,
            device_id_type=MESH,
        )

    def send(k, source, target, condition=None, own=False):
        slot = slots[k]
        slots[k] += 1
        guarded(condition, lambda: copy_of(k, source, target, slot, own).start())
        sent.append((k, source, target, slot, condition, own))

    def arrive(k, source, condition=None):
        guarded(condition, lambda: copy_of(k, source, me, 0).wait_recv())

    links = {
        "left": (place.at(z - 1), z > 0),
        "right": (place.at(z + 1), z < last),
        "p": (place.near(z, 1, 0), None),
        "q": (place.near(z, 0, 1), None),
        "core": (place.at(z, 0, 0, 1), None),
    }

    def forward(k, source, ways, condition=None, own=False):
        for way in ways:
            target, open_way = links[way]
            send(k, source, target, both(condition, open_way), own)

    def spots(offset):
        if offset == 0:
            return [(z, None, ("left", "right"))]
        return [
            (z - offset, z >= offset, ("right",)),
            (z + offset, z + offset <= last, ("left",)),
        ]

    def take(k, source, condition, ways):
        arrive(k, source, condition)
        forward(k, source, ways, condition)

    def step_z_first(k, step):
        if step == 0:
            forward(k, me, ("left", "right", "q", "p", "core"), own=True)
            return
        if step < place.lines:
            for spot, there, ways in spots(step):
                take(k, place.near(spot, 0, 0), there, ways + ("q", "p", "core"))
        if 0 <= step - 1 < place.lines:
            for spot, there, _ in spots(step - 1):
                take(k, place.near(spot, 1, 0), there, ("q", "core"))
                take(k, place.near(spot, 0, 1), there, ("core",))
        if 0 <= step - 2 < place.lines:
            for spot, there, _ in spots(step - 2):
                take(k, place.near(spot, 1, 1), there, ("core",))

    def step_z_second(k, step):
        if step == 0:
            forward(k, me, ("q", "left", "right", "p", "core"), own=True)
            return
        if step == 1:
            take(k, place.near(z, 0, 1), None, ("left", "right", "p", "core"))
        if step < place.lines:
            for spot, there, ways in spots(step):
                take(k, place.near(spot, 0, 0), there, ways + ("p", "core"))
        if 1 <= step - 1 < place.lines:
            for spot, there, ways in spots(step - 1):
                take(k, place.near(spot, 0, 1), there, ways + ("p", "core"))
        if 0 <= step - 1 < place.lines:
            for spot, there, _ in spots(step - 1):
                take(k, place.near(spot, 1, 0), there, ("core",))
        if 0 <= step - 2 < place.lines:
            for spot, there, _ in spots(step - 2):
                take(k, place.near(spot, 1, 1), there, ("core",))

    own_copies = [
        pltpu.make_async_copy(ins[k], view(k, me), own_sem.at[k]) for k in range(count)
    ]
    def from_core(k):
        for spot in range(place.lines):
            for p in range(2):
                for q in range(2):
                    arrive(k, place.across(spot, p, q))

    def read_small():
        copy = pltpu.make_async_copy(outs[tiny], small_here, small_sem)
        copy.start()
        copy.wait()

    def compute(part):
        groups = outs[conv].shape[1]
        if part == 0:
            read_small()
            project()
        elif part < 4:
            convolve(groups * (part - 1) // 3, groups * part // 3)
        else:
            leave()

    for name, kind, step in GATHER_PLAN:
        if name == "step":
            k = KINDS.index(kind)
            (step_z_second if kind == "blocks" else step_z_first)(k, step)
            if step == 0:
                own_copies[k].start()
        elif name == "core":
            from_core(KINDS.index(kind))
            own_copies[KINDS.index(kind)].wait()
        elif name == "enter":
            enter()
        else:
            compute(step)
    from_core(KINDS.index("blocks"))
    own_copies[KINDS.index("blocks")].wait()
    for k, source, target, slot, condition, own in sent:
        guarded(
            condition,
            lambda k=k, source=source, target=target, slot=slot, own=own: copy_of(
                k, source, target, slot, own
            ).wait_send(),
        )


def full_shapes(sizes, shapes):
    dp_size, group_size = sizes
    conv, small, blocks = shapes
    return [
        (group_size, dp_size * conv[0]) + conv[1:],
        (dp_size, group_size) + small,
        (group_size * blocks[0], dp_size * blocks[1], blocks[2]),
    ]


def gather_weights(sizes, shapes, taps, raw, features, feature_norm, vectors):
    low, out = jnp.bfloat16, jax.ShapeDtypeStruct
    full = full_shapes(sizes, shapes)
    frames, width = features.shape
    count, devices = len(shapes), sizes[0] * sizes[1]
    dma = pltpu.SemaphoreType.DMA
    return pl.pallas_call(
        functools.partial(gather_kernel, sizes, shapes, taps),
        out_shape=[out(shape, low) for shape in full]
        + front_shapes(frames, width)
        + [out((frames, 1), jnp.float32), out(raw[-1].shape, low)],
        in_specs=[VMEM] * (len(raw) + 3),
        out_specs=[HBM] * count + [VMEM] * 9,
        scratch_shapes=[pltpu.VMEM(shape, low) for shape in shapes]
        + [pltpu.VMEM(full[1], low)]
        + front_scratch(full[0], frames)
        + [
            dma((count, 3 * devices)),
            dma((count, devices)),
            dma((count,)),
            dma,
        ],
        name="gather_front",
        compiler_params=pltpu.CompilerParams(
            collective_id=0, has_side_effects=True, vmem_limit_bytes=VMEM_LIMIT
        ),
    )(*raw, features, feature_norm, vectors)


class StatRows:
    def __init__(self, sizes, stats_in, stats_out, sems):
        self.place = Place(*sizes)
        self.members, _, self.rows, _ = stats_in.shape
        self.owners = Owners(self.place, self.members)
        self.stats_in, self.stats_out = stats_in, stats_out
        self.send_sem, self.recv_sem, self.own_sem = sems

    def spot(self, other):
        return pl.ds(pl.multiple_of(other * self.rows, self.rows), self.rows)

    def away(self, member, side):
        place = self.place
        return pltpu.make_async_remote_copy(
            src_ref=self.stats_in.at[member, side],
            dst_ref=self.stats_out.at[self.spot(place.dp)],
            send_sem=self.send_sem.at[member, side],
            recv_sem=self.recv_sem.at[place.dp],
            device_id=(self.owners.of(member), place.x * 2 + side),
            device_id_type=MESH,
        )

    def here(self, member, side):
        return pltpu.make_async_copy(
            self.stats_in.at[member, side], self.stats_out.at[self.spot(self.place.dp)], self.own_sem
        )

    def each(self, away, here):
        place = self.place
        for member in range(self.members):
            for side in range(2):
                mine = (place.dp == self.owners.of(member)) & (place.core == side)
                pl.when(jnp.logical_not(mine))(functools.partial(away, member, side))
                pl.when(mine)(functools.partial(here, member, side))

    def start(self):
        self.each(lambda m, s: self.away(m, s).start(), lambda m, s: self.here(m, s).start())

    def finish(self):
        place = self.place
        self.each(lambda m, s: self.away(m, s).wait_send(), lambda m, s: self.here(m, s).wait())

        @pl.when(self.owners.here)
        def _():
            for other in range(place.dp_size):

                @pl.when((place.dp != other) | (place.group != self.owners.group))
                def _(other=other):
                    pltpu.make_async_remote_copy(
                        src_ref=self.stats_in.at[0, 0],
                        dst_ref=self.stats_out.at[self.spot(other)],
                        send_sem=self.send_sem.at[0, 0],
                        recv_sem=self.recv_sem.at[other],
                        device_id=(place.dp, place.group),
                        device_id_type=MESH,
                    ).wait_recv()


def shift_right(values, by):
    if by == 0:
        return values
    parts = []
    for first in range(0, values.shape[1], CLIP):
        part = values[:, first : first + CLIP]
        lane = lax.broadcasted_iota(jnp.int32, part.shape, 1)
        turned = pltpu.roll(part, by % CLIP, 1)
        inside = lane >= by if by > 0 else lane < CLIP + by
        parts.append(jnp.where(inside, turned, 0.0))
    return jnp.concatenate(parts, 1)


def place_windows(hidden, windows, taps):
    channels = hidden.shape[0]
    runs, half = taps // STRIDE, taps // STRIDE // 2
    for run in range(runs):
        by = STRIDE * (half - 1 - run) if run < half else -STRIDE * (run - half)
        windows[run * channels : (run + 1) * channels, :] = shift_right(hidden, by).astype(
            jnp.bfloat16
        )


def conv_group(hidden, weight_at, windows, taps, shape):
    channels = hidden.shape[0]
    chunks, _, _, chunk = shape
    place_windows(hidden, windows, taps)
    total = None
    for side in range(2):
        part = None
        for index in range(side * chunks // 2, (side + 1) * chunks // 2):
            term = dot(weight_at(index), windows[index * chunk : (index + 1) * chunk, :])
            part = term if part is None else part + term
        for offset in range(STRIDE):
            by = STRIDE - offset if side == 0 else -offset
            moved = shift_right(part[offset * channels : (offset + 1) * channels], by)
            total = moved if total is None else total + moved
    return total


def conv_group_back(hidden, grad, weight_at, put, windows, moved, taps, shape):
    channels = hidden.shape[0]
    chunks, _, _, chunk = shape
    half, runs = taps // STRIDE // 2, chunk // channels
    place_windows(hidden, windows, taps)
    total = None
    for side in range(2):
        for offset in range(STRIDE):
            by = offset - STRIDE if side == 0 else offset
            moved[offset * channels : (offset + 1) * channels, :] = shift_right(grad, by).astype(
                jnp.bfloat16
            )
        for index in range(side * chunks // 2, (side + 1) * chunks // 2):
            put(
                index,
                dot_nt(moved[...], windows[index * chunk : (index + 1) * chunk, :]).astype(
                    jnp.bfloat16
                ),
            )
            turned = dot_tn(weight_at(index), moved[...])
            for step in range(runs):
                run = index * runs + step
                by = -STRIDE * (half - 1 - run) if run < half else STRIDE * (run - half)
                part = shift_right(turned[step * channels : (step + 1) * channels], by)
                total = part if total is None else total + part
    return total


def over_rows(total, tile, action):
    def step(index, _):
        action(pl.ds(pl.multiple_of(index * tile, tile), tile))
        return 0

    lax.fori_loop(0, total // tile, step, 0, unroll=2)


def dot(one, two):
    return jnp.dot(one, two, preferred_element_type=jnp.float32)


def dot_nt(one, two):
    return lax.dot_general(one, two, (((1,), (1,)), ((), ())), preferred_element_type=jnp.float32)


def dot_tn(one, two):
    return lax.dot_general(one, two, (((0,), (0,)), ((), ())), preferred_element_type=jnp.float32)


def norm_parts(values):
    average = jnp.mean(values, -1, keepdims=True)
    centred = values - average
    inverse = lax.rsqrt(jnp.mean(centred * centred, -1, keepdims=True) + 1e-05)
    return centred * inverse, inverse


def norm_back(upstream, unit, inverse, gain):
    scaled = upstream * gain
    along = jnp.mean(scaled * unit, -1, keepdims=True)
    return inverse * (scaled - jnp.mean(scaled, -1, keepdims=True) - unit * along)


def gelu_pair(values):
    below = 0.5 + 0.5 * lax.erf(values * 0.7071067811865476)
    density = jnp.exp(values * values * -0.5) * 0.3989422804014327
    return values * below, below + values * density


def add_row(ref, row, values):
    ref[row : row + 1, :] += jnp.sum(values, 0, keepdims=True)


def front_compute(taps, refs, outs, scratch):
    features, mask, feature_norm, vectors, small, kernel = refs
    feature_unit, normed, hidden_t, encoded, encoder_unit, encoder_inverse, slope = outs
    held, windows, hidden, out_t, load_sem = scratch
    frames = features.shape[0]
    groups = kernel.shape[1]
    channels = hidden_t.shape[0] // groups

    def load(group):
        return pltpu.make_async_copy(kernel.at[:, group], held.at[:, group], load_sem.at[group])

    def enter():
        def one(at):
            unit, _ = norm_parts(features[at, :].astype(jnp.float32))
            feature_unit[at, :] = unit
            scaled = unit * feature_norm[0:1, :] + feature_norm[1:2, :]
            normed[at, :] = scaled.astype(jnp.bfloat16)

        over_rows(frames, 32, one)

    def project():
        for group in range(groups):
            load(group).start()
        normed_t = normed[...].T
        parts, columns = small.shape[0], small.shape[1]
        third = D // columns
        for group in range(columns):
            for first, size in ((0, 128), (128, third - 128)):
                row = first // 2
                part = small[:, group, row : row + 64, :].reshape(parts * 64, 128)
                at = group * third + first
                out_t[at : at + size, :] = dot_tn(part, normed_t)[:size]
        hidden[...] = jnp.where(mask[...] > 0, vectors[0:1, :], out_t[...].T)
        hidden_t[...] = hidden[...].T.astype(jnp.bfloat16)

    def one_group(group, _):
        load(group).wait()
        at = pl.ds(pl.multiple_of(group * channels, channels), channels)
        out_t[at, :] = conv_group(
            hidden_t[at, :].astype(jnp.float32),
            lambda index: held[index, group],
            windows,
            taps,
            kernel.shape,
        )
        return 0

    def convolve(first, last):
        lax.fori_loop(first, last, one_group, 0)

    def leave():
        slope[...] = out_t[...].T

        def one(at):
            active, derivative = gelu_pair(slope[at, :])
            slope[at, :] = derivative
            unit, inverse = norm_parts(hidden[at, :] + active)
            encoder_unit[at, :] = unit
            encoder_inverse[at, :] = inverse
            encoded[at, :] = unit * vectors[1:2, :] + vectors[2:3, :]

        over_rows(frames, 32, one)

    return enter, project, convolve, leave


def front_kernel(taps, *refs):
    enter, project, convolve, leave = front_compute(taps, refs[:6], refs[6:13], refs[13:])
    enter()
    project()
    convolve(0, refs[5].shape[1])
    leave()


def front_shapes(frames, width):
    out, full, low = jax.ShapeDtypeStruct, jnp.float32, jnp.bfloat16
    return [
        out((frames, width), full),
        out((frames, width), low),
        out((D, frames), low),
        out((frames, D), full),
        out((frames, D), full),
        out((frames, 1), full),
        out((frames, D), full),
    ]


def front_scratch(kernel_shape, frames):
    chunks, groups, rows, chunk = kernel_shape
    return [
        pltpu.VMEM(kernel_shape, jnp.bfloat16),
        pltpu.VMEM((chunks * chunk, frames), jnp.bfloat16),
        pltpu.VMEM((frames, D), jnp.float32),
        pltpu.VMEM((D, frames), jnp.float32),
        pltpu.SemaphoreType.DMA((groups,)),
    ]


def front(features, mask, feature_norm, vectors, small, kernel, taps):
    frames, width = features.shape
    return pl.pallas_call(
        functools.partial(front_kernel, taps),
        out_shape=front_shapes(frames, width),
        in_specs=[VMEM] * 5 + [HBM],
        out_specs=[VMEM] * 7,
        scratch_shapes=front_scratch(kernel.shape, frames),
        name="front",
        compiler_params=pltpu.CompilerParams(vmem_limit_bytes=VMEM_LIMIT),
    )(features, mask, feature_norm, vectors, small, kernel)


def trunk_kernel(sizes, *refs):
    refs = list(refs)
    rows_moved = None
    if sizes is not None:
        stats_in, stats_out = refs.pop(6), refs.pop(12)
        rows_moved = StatRows(sizes, stats_in, stats_out, refs[-3:])
        refs = refs[:-3]
    (
        encoded, mask, labels, vectors, small, blocks,
        encoded_grad, block_grad, head_grad, center_grad_t, rows_out, counted,
        head, table, centers, held, made, low, triple, attention, mixed, unit_one, inverse_one, middle, middle_low,
        active, slope, unit_two, inverse_two, work, work_low, flow_low, triple_grad, turned,
        load_sem, save_sem,
    ) = refs
    frames = encoded.shape[0]
    count = blocks.shape[0]
    ups = (count - 4) // 2
    tile = 32
    pairs = D // 128

    def load(block):
        return pltpu.make_async_copy(blocks.at[block], held.at[block], load_sem.at[block])

    def save(block):
        return pltpu.make_async_copy(made.at[block], block_grad.at[block], save_sem.at[block])

    for block in range(count):
        load(block).start()
    if rows_moved is not None:
        greet(rows_moved.place)
        rows_moved.start()
    rows_out[...] = jnp.zeros_like(rows_out)
    parts, columns = small.shape[0], small.shape[1]
    notes = small[:, :, 224:240, :].astype(jnp.float32)
    first = lax.broadcasted_iota(jnp.int32, notes.shape, 2) == 0
    first &= lax.broadcasted_iota(jnp.int32, notes.shape, 3) == CLUSTER_ROWS
    notes = jnp.sum(jnp.where(first, notes, 0.0), (0, 1))
    masked = jnp.sum(jnp.sum(notes, 1, keepdims=True), 0, keepdims=True)
    counted[...] = masked

    def to_inputs(at):
        low[at, :] = encoded[at, :].astype(jnp.bfloat16)

    over_rows(frames, tile, to_inputs)

    def first_three(block, _):
        load(block).wait()
        triple[block] = dot(low[...], held[block]).astype(jnp.bfloat16)
        return 0

    lax.fori_loop(0, 3, first_three, 0)
    lane = lax.broadcasted_iota(jnp.int32, (CLIP, 128), 1)
    even = lane < HEAD

    def apart(values):
        zero = jnp.zeros_like(values)
        return jnp.concatenate([jnp.where(even, values, zero), jnp.where(even, zero, values)], 0)

    def beside(values):
        return jnp.concatenate([values[:CLIP], values[CLIP:]], 1)

    def spot(index):
        at = pl.ds(pl.multiple_of(index // pairs * CLIP, CLIP), CLIP)
        return at, pl.ds(pl.multiple_of(index % pairs * 128, 128), 128)

    def attend(index, _):
        at, lanes = spot(index)
        query, keys, values = triple[0, at, lanes], triple[1, at, lanes], triple[2, at, lanes]
        scores = dot_nt(apart(query), keys) * HEAD ** (-0.5)
        raised = jnp.exp(scores - jnp.max(scores, -1, keepdims=True))
        full = raised / jnp.sum(raised, -1, keepdims=True)
        attention[index] = full
        mixed[at, lanes] = dot(beside(full.astype(jnp.bfloat16)), apart(values)).astype(jnp.bfloat16)
        return 0

    lax.fori_loop(0, frames // CLIP * pairs, attend, 0, unroll=pairs)
    load(3).wait()
    work[...] = dot(mixed[...], held[3])

    def first_norm(at):
        unit, inverse = norm_parts(encoded[at, :] + work[at, :])
        unit_one[at, :] = unit
        inverse_one[at, :] = inverse
        value = unit * vectors[3:4, :] + vectors[4:5, :]
        middle[at, :] = value
        middle_low[at, :] = value.astype(jnp.bfloat16)

    over_rows(frames, tile, first_norm)

    def expand(step, _):
        load(4 + step).wait()
        slope[step] = dot(middle_low[...], held[4 + step])

        def bend(at):
            value, derivative = gelu_pair(slope[step, at, :])
            active[step, at, :] = value.astype(jnp.bfloat16)
            slope[step, at, :] = derivative

        over_rows(frames, tile, bend)
        return 0

    lax.fori_loop(0, ups, expand, 0)

    def contract(step, _):
        load(4 + ups + step).wait()
        middle[...] += dot(active[step], held[4 + ups + step])
        return 0

    lax.fori_loop(0, ups, contract, 0)

    def second_norm(at):
        unit, inverse = norm_parts(middle[at, :])
        unit_two[at, :] = unit
        inverse_two[at, :] = inverse
        flow_low[at, :] = (unit * vectors[5:6, :] + vectors[6:7, :]).astype(jnp.bfloat16)

    over_rows(frames, tile, second_norm)
    table[...] = jnp.zeros_like(table)
    for group in range(columns):
        across = slice(group * 128, group * 128 + 128)
        head[:, across] = small[:, group, 128:224, :].reshape(parts * 96, 128)
        for part in range(parts):
            row = part // 2 * 128 + part % 2 * 32
            table[row : row + 32, across] = small[part, group, 224:256, :].astype(jnp.float32)
    real = lax.broadcasted_iota(jnp.int32, (1, table.shape[1]), 1) % 128 < CLUSTER_ROWS
    table[...] = jnp.where(real, table[...], 0.0)
    size = lax.rsqrt(jnp.sum(table[...] * table[...], 0, keepdims=True) + 1e-06)
    centers[...] = (table[...] * size).astype(jnp.bfloat16)
    embedded = dot(flow_low[...], head[...])
    length = lax.rsqrt(jnp.sum(embedded * embedded, -1, keepdims=True) + 1e-06)
    unit_low = (embedded * length).astype(jnp.bfloat16)
    logits = jnp.where(real, dot(unit_low, centers[...]) * inv_temp, -1e30)
    top = jnp.max(logits, -1, keepdims=True)
    raised = jnp.exp(logits - top)
    amount = jnp.sum(raised, -1, keepdims=True)
    columns_of = labels[...]
    for group in range(1, columns):
        columns_of = columns_of + jnp.where(labels[...] >= group * CLUSTER_ROWS, 128 - CLUSTER_ROWS, 0)
    choose = columns_of == lax.broadcasted_iota(jnp.int32, logits.shape, 1)
    target = jnp.sum(jnp.where(choose, logits, 0.0), -1, keepdims=True)
    losses = mask[...] * (jnp.log(amount) + top - target)
    rows_out[7:8, :] = jnp.broadcast_to(jnp.sum(losses, 0, keepdims=True), (1, D))
    logit_grad = (
        (raised / amount - choose.astype(jnp.float32)) * (mask[...] * (1.0 / masked))
    ).astype(jnp.bfloat16)
    unit_grad = dot_nt(logit_grad, centers[...]) * inv_temp
    spread = dot_tn(unit_low, logit_grad) * inv_temp
    shared = jnp.sum(spread * table[...], 0, keepdims=True)
    spread = size * spread - table[...] * (size * size * size * shared)
    for group in range(columns):
        center_grad_t[group * 64 : group * 64 + 64, :] = spread[group * 128 : group * 128 + 64, :]
    along = jnp.sum(unit_grad * embedded, -1, keepdims=True)
    embedded_grad = (
        length * unit_grad - embedded * (length * length * length * along)
    ).astype(jnp.bfloat16)
    work[...] = dot_nt(embedded_grad, head[...])
    head_grad[...] = dot_tn(flow_low[...], embedded_grad).astype(jnp.bfloat16)

    def second_back(at):
        upstream = work[at, :]
        add_row(rows_out, 5, upstream * unit_two[at, :])
        add_row(rows_out, 6, upstream)
        value = norm_back(upstream, unit_two[at, :], inverse_two[at, :], vectors[5:6, :])
        middle[at, :] = value
        flow_low[at, :] = value.astype(jnp.bfloat16)

    over_rows(frames, tile, second_back)
    turned[...] = middle_low[...].T

    def feed_back(step, _):
        work[...] = dot_nt(flow_low[...], held[4 + ups + step])
        made[4 + ups + step] = dot_tn(active[step], flow_low[...]).astype(jnp.bfloat16)
        save(4 + ups + step).start()

        def bend(at):
            work_low[at, :] = (work[at, :] * slope[step, at, :]).astype(jnp.bfloat16)

        over_rows(frames, tile, bend)
        made[4 + step] = dot(turned[...], work_low[...]).astype(jnp.bfloat16)
        save(4 + step).start()
        middle[...] += dot_nt(work_low[...], held[4 + step])
        return 0

    lax.fori_loop(0, ups, feed_back, 0)

    def first_back(at):
        upstream = middle[at, :]
        add_row(rows_out, 3, upstream * unit_one[at, :])
        add_row(rows_out, 4, upstream)
        value = norm_back(upstream, unit_one[at, :], inverse_one[at, :], vectors[3:4, :])
        middle[at, :] = value
        flow_low[at, :] = value.astype(jnp.bfloat16)

    over_rows(frames, tile, first_back)
    made[3] = dot_tn(mixed[...], flow_low[...]).astype(jnp.bfloat16)
    save(3).start()
    work_low[...] = dot_nt(flow_low[...], held[3]).astype(jnp.bfloat16)

    def attend_back(index, _):
        at, lanes = spot(index)
        query, keys, values = triple[0, at, lanes], triple[1, at, lanes], triple[2, at, lanes]
        upstream = apart(work_low[at, lanes])
        full = attention[index]
        full_grad = dot_nt(upstream, values)
        triple_grad[2, at, lanes] = dot_tn(full.astype(jnp.bfloat16), upstream).astype(jnp.bfloat16)
        along = jnp.sum(full * full_grad, -1, keepdims=True)
        score_grad = (full * (full_grad - along)).astype(jnp.bfloat16)
        triple_grad[0, at, lanes] = (
            dot(beside(score_grad), apart(keys)) * HEAD ** (-0.5)
        ).astype(jnp.bfloat16)
        triple_grad[1, at, lanes] = (
            dot_tn(score_grad, apart(query)) * HEAD ** (-0.5)
        ).astype(jnp.bfloat16)
        return 0

    lax.fori_loop(0, frames // CLIP * pairs, attend_back, 0, unroll=pairs)
    turned[...] = low[...].T

    def last_three(block, _):
        made[block] = dot(turned[...], triple_grad[block]).astype(jnp.bfloat16)
        save(block).start()
        middle[...] += dot_nt(triple_grad[block], held[block])
        return 0

    lax.fori_loop(0, 3, last_three, 0)
    encoded_grad[...] = middle[...]
    if rows_moved is not None:
        rows_moved.finish()
    for block in range(count):
        save(block).wait()


def trunk(encoded, mask, labels, vectors, small, blocks, sizes=None, stats_low=None):
    frames, count = encoded.shape[0], blocks.shape[0]
    ups, columns = (count - 4) // 2, small.shape[1] * 128
    full, low = jnp.float32, jnp.bfloat16
    out = jax.ShapeDtypeStruct
    wide, wide_low = pltpu.VMEM((frames, D), full), pltpu.VMEM((frames, D), low)
    column = pltpu.VMEM((frames, 1), full)
    more_in, more_out, sems, settings = [], [], [], {}
    if sizes is not None:
        dma = pltpu.SemaphoreType.DMA
        more_in, more_out = [stats_low], [out((D, D), low)]
        sems = [dma((stats_low.shape[0], 2)), dma((sizes[0],)), dma]
        settings = {"collective_id": 3, "has_side_effects": True}
    return pl.pallas_call(
        functools.partial(trunk_kernel, sizes),
        out_shape=[
            out((frames, D), full),
            out(blocks.shape, low),
            out((D, columns), low),
            out((columns // 2, columns), full),
            out((8, D), full),
            out((1, 1), full),
        ]
        + more_out,
        in_specs=[VMEM] * 5 + [HBM] * (1 + len(more_in)),
        out_specs=[VMEM, HBM] + [VMEM] * 4 + [HBM] * len(more_out),
        scratch_shapes=[
            pltpu.VMEM((D, columns), low),
            pltpu.VMEM((columns, columns), full),
            pltpu.VMEM((columns, columns), low),
            pltpu.VMEM(blocks.shape, low),
            pltpu.VMEM(blocks.shape, low),
            wide_low,
            pltpu.VMEM((3, frames, D), low),
            pltpu.VMEM((frames // CLIP * D // 128, 2 * CLIP, CLIP), full),
            wide_low,
            wide,
            column,
            wide,
            wide_low,
            pltpu.VMEM((ups, frames, D), low),
            pltpu.VMEM((ups, frames, D), full),
            wide,
            column,
            wide,
            wide_low,
            wide_low,
            pltpu.VMEM((3, frames, D), low),
            pltpu.VMEM((D, frames), low),
            pltpu.SemaphoreType.DMA((count,)),
            pltpu.SemaphoreType.DMA((count,)),
        ]
        + sems,
        name="trunk",
        compiler_params=pltpu.CompilerParams(vmem_limit_bytes=VMEM_LIMIT, **settings),
    )(encoded, mask, labels, vectors, small, blocks, *more_in)


LOSS_ROW = 7


class Owners:
    def __init__(self, place, members):
        self.place, self.members = place, members
        self.first = (place.dp_size - 2 * members) // 2
        index = place.dp - self.first
        self.here = (index >= 0) & (index < 2 * members)
        self.group = place.x * 2 + index // members
        self.member = index % members

    def of(self, member):
        return self.first + self.place.core * self.members + member

    def to_rows(self, other, remote_action, local_action):
        place = self.place
        away = (place.dp != other) | (place.group != self.group)
        pl.when(away)(functools.partial(remote_action, other))
        pl.when(jnp.logical_not(away))(local_action)


class Reducer:
    def __init__(self, place, shapes, local, refs, sems):
        self.place, self.shapes, self.local = place, shapes, local
        self.z, self.lines, self.last = place.z, place.lines, place.lines - 1
        self.blocks = KINDS.index("blocks")
        self.rest = [k for k in range(len(KINDS)) if k != self.blocks]
        self.crossed, self.first_in, self.second_in, self.line_in = refs[:4]
        self.held, self.source = refs[4:]
        (
            self.load_sem, self.cross_send, self.cross_recv, self.first_send, self.first_recv,
            self.second_send, self.second_recv, self.left_send, self.left_recv, self.right_send,
            self.right_recv,
        ) = sems
        self.p_mate, self.q_mate = place.near(self.z, 1, 0), place.near(self.z, 0, 1)
        self.c_mate = place.at(self.z, 0, 0, 1)
        self.left, self.right = place.at(self.z - 1), place.at(self.z + 1)

    def remote(self, source, target, send, recv, device):
        return pltpu.make_async_remote_copy(
            src_ref=source,
            dst_ref=target,
            send_sem=send,
            recv_sem=recv,
            device_id=device,
            device_id_type=MESH,
        )

    def load_of(self, p, q, spot):
        k = self.blocks
        dp, group = self.place.near(spot, p, q)
        return pltpu.make_async_copy(
            piece_at("blocks", self.source[k], dp, group, self.shapes[k]),
            self.held.at[p, spot],
            self.load_sem.at[p, q, spot],
        )

    def cross_of(self, k, p, q, spot):
        dp, group = self.place.across(spot, p, q)
        return self.remote(
            piece_at(KINDS[k], self.source[k], dp, group, self.shapes[k]),
            self.crossed[k].at[p, q, spot],
            self.cross_send.at[k, p, q, spot],
            self.cross_recv.at[k, p, q, spot],
            self.c_mate,
        )

    def own(self, k, p, q, spot):
        if k == self.blocks:
            self.load_of(p, q, spot).wait()
            return f32(self.held, (p, spot))
        dp, group = self.place.near(spot, p, q)
        return piece_at(KINDS[k], self.source[k], dp, group, self.shapes[k])[...].astype(jnp.float32)

    def met(self, k, p, q, spot):
        own = self.own(k, p, q, spot)
        self.cross_of(k, p, q, spot).wait_recv()
        return own + f32(self.crossed[k], (p, q, spot))

    def turn(self, index):
        odd = index % 2
        return (1 - odd) * (self.last - index // 2) + odd * (index // 2)

    def first_out(self, k, p, spot):
        return self.remote(
            self.crossed[k].at[p, 1, spot],
            self.first_in[k].at[p, spot],
            self.first_send.at[k, p, spot],
            self.first_recv.at[k, p, spot],
            self.q_mate,
        )

    def stage_one(self, k, index):
        p, spot = 1 - index // self.lines, self.turn(index % self.lines)
        self.crossed[k][p, 1, spot] = self.met(k, p, 1, spot).astype(jnp.bfloat16)
        self.first_out(k, p, spot).start()
        if k == self.blocks:
            self.load_of(p, 0, spot).start()

    def joined(self, k, p, spot):
        total = self.met(k, p, 0, spot)
        self.first_out(k, p, spot).wait_recv()
        return total + f32(self.first_in[k], (p, spot))

    def second_out(self, k, spot):
        return self.remote(
            self.crossed[k].at[1, 0, spot],
            self.second_in[k].at[spot],
            self.second_send.at[k, spot],
            self.second_recv.at[k, spot],
            self.p_mate,
        )

    def stage_two(self, k, index):
        spot = self.turn(index)
        self.crossed[k][1, 0, spot] = self.joined(k, 1, spot).astype(jnp.bfloat16)
        self.second_out(k, spot).start()

    def line_total(self, k, spot):
        total = self.joined(k, 0, spot)
        self.second_out(k, spot).wait_recv()
        return total + f32(self.second_in[k], (spot,))

    def line_out(self, k, spot, way):
        if way == "right":
            send, recv, device, slot = self.right_send, self.left_recv, self.right, spot
        else:
            send, recv, device = self.left_send, self.right_recv, self.left
            ends = (self.last - (self.z - 1 - spot)) // self.last
            slot = spot + ends * (self.lines - spot)
        return self.remote(
            self.crossed[k].at[0, 0, spot],
            self.line_in[k].at[slot],
            send.at[k, spot],
            recv.at[k, spot],
            device,
        )

    def came_in(self, k, spot, way):
        recv = self.left_recv if way == "right" else self.right_recv
        send = self.right_send if way == "right" else self.left_send
        return self.remote(
            self.crossed[k].at[0, 0, spot],
            self.line_in[k].at[spot],
            send.at[k, spot],
            recv.at[k, spot],
            self.c_mate,
        )

    def pass_on(self, k, spot, way, inner):
        z = self.z
        if way == "right":
            here = (z < spot) & ((z > 0) if inner else (z == 0))
        else:
            here = (z > spot) & ((z < self.last) if inner else (z == self.last))

        @pl.when(here)
        def _():
            total = self.line_total(k, spot)
            if inner:
                self.came_in(k, spot, way).wait_recv()
                total = total + f32(self.line_in[k], (spot,))
            self.crossed[k][0, 0, spot] = total.astype(jnp.bfloat16)
            self.line_out(k, spot, way).start()

    def line_step(self, k, step, inner):
        self.pass_on(k, self.last - step, "right", inner)
        self.pass_on(k, step, "left", inner)

    def line_end(self, k, out):
        z = self.z
        out[...] = self.line_total(k, z)

        @pl.when(z > 0)
        def _():
            self.came_in(k, z, "right").wait_recv()
            out[...] += f32(self.line_in[k], (z,))

        @pl.when(z < self.last)
        def _():
            self.came_in(k, z, "left").wait_recv()
            out[...] += f32(self.line_in[k], (self.lines,))

    def drain(self):
        for k in range(len(KINDS)):

            def one(spot, _, k=k):
                for p in range(2):
                    for q in range(2):
                        self.cross_of(k, p, q, spot).wait_send()
                    self.first_out(k, p, spot).wait_send()
                self.second_out(k, spot).wait_send()

                @pl.when(self.z < spot)
                def _():
                    self.line_out(k, spot, "right").wait_send()

                @pl.when(self.z > spot)
                def _():
                    self.line_out(k, spot, "left").wait_send()

                return 0

            lax.fori_loop(0, self.lines, one, 0)


def f32(ref, at):
    return ref[at].astype(jnp.float32)


def back_compute(taps, refs, made, small_made, rows, scratch, hook):
    (
        encoded_grad, mask, vectors, small, feature_unit, normed, hidden_t,
        encoder_unit, encoder_inverse, slope, trunk_rows, head_grad, center_grad_t, kernel,
    ) = refs
    slots, windows, moved, grad, grad_t, through, through_t, load_sem = scratch
    frames, width = feature_unit.shape
    groups = kernel.shape[1]
    channels = hidden_t.shape[0] // groups

    def load(group):
        slot = group % 2
        return pltpu.make_async_copy(kernel.at[:, group], slots.at[slot], load_sem.at[slot])

    def begin():
        load(0).start()
        rows[...] = jnp.zeros_like(rows)
        rows[0:8, :] = trunk_rows[...]
        over_rows(frames, 32, enter)
        grad_t[...] = through[...].T.astype(jnp.bfloat16)

    def enter(at):
        upstream = encoded_grad[at, :]
        add_row(rows, 1, upstream * encoder_unit[at, :])
        add_row(rows, 2, upstream)
        value = norm_back(upstream, encoder_unit[at, :], encoder_inverse[at, :], vectors[1:2, :])
        grad[at, :] = value
        through[at, :] = value * slope[at, :]

    def one_group(group, _):
        pl.when(group + 1 < groups)(lambda: load(group + 1).start())
        load(group).wait()
        at = pl.ds(pl.multiple_of(group * channels, channels), channels)

        def put(index, value):
            made[index, group] = value

        through_t[at, :] = conv_group_back(
            hidden_t[at, :].astype(jnp.float32),
            grad_t[at, :].astype(jnp.float32),
            lambda index: slots[group % 2, index],
            put,
            windows,
            moved,
            taps,
            kernel.shape,
        )
        hook(group)
        return 0

    def convolve(first, last):
        lax.fori_loop(first, last, one_group, 0)

    def leave(at):
        total = grad[at, :] + through[at, :]
        inside = mask[at, :] > 0
        add_row(rows, 0, jnp.where(inside, total, 0.0))
        grad[at, :] = jnp.where(inside, 0.0, total)

    def finish():
        through[...] = through_t[...].T
        over_rows(frames, 32, leave)
        grad_t[...] = grad[...].T.astype(jnp.bfloat16)
        normed_t = normed[...].T
        parts, columns = small.shape[0], small.shape[1]
        third = D // columns
        total = None
        for group in range(columns):
            one = grad_t[group * third : group * third + 128, :]
            two = grad_t[group * third + 128 : (group + 1) * third, :]
            lane = third - 128
            wide = dot_nt(normed_t, one).astype(jnp.bfloat16)
            thin = dot_nt(normed_t, two).astype(jnp.bfloat16)
            small_made[:, group, 0:64, :] = wide.reshape(parts, 64, 128)
            small_made[:, group, 64:128, :] = jnp.concatenate(
                [thin, jnp.zeros((thin.shape[0], 128 - lane), jnp.bfloat16)], 1
            ).reshape(parts, 64, 128)
            small_made[:, group, 128:224, :] = head_grad[:, group * 128 : group * 128 + 128].reshape(
                parts, 96, 128
            )
            small_made[:, group, 224:256, :] = (
                center_grad_t[:, group * 128 : group * 128 + 128]
                .astype(jnp.bfloat16)
                .reshape(parts, 32, 128)
            )
            first = small[:, group, 0:64, :].reshape(parts * 64, 128)
            second = small[:, group, 64:128, :].reshape(parts * 64, 128)[:, :lane]
            term = dot(first, one) + dot(second, two)
            total = term if total is None else total + term
        normed_grad = total.T
        rows[8:9, 0:width] = jnp.sum(normed_grad * feature_unit[...], 0, keepdims=True)
        rows[9:10, 0:width] = jnp.sum(normed_grad, 0, keepdims=True)

    return begin, convolve, finish


def back_scratch(kernel_shape, frames):
    chunks, groups, rows, chunk = kernel_shape
    full, low = jnp.float32, jnp.bfloat16
    return [
        pltpu.VMEM((2, chunks, rows, chunk), low),
        pltpu.VMEM((chunks * chunk, frames), low),
        pltpu.VMEM((rows, frames), low),
        pltpu.VMEM((frames, D), full),
        pltpu.VMEM((D, frames), low),
        pltpu.VMEM((frames, D), full),
        pltpu.VMEM((D, frames), full),
        pltpu.SemaphoreType.DMA((2,)),
    ]


BACK_INPUTS = 14


def back_kernel(taps, *refs):
    made, small_made, rows = refs[BACK_INPUTS : BACK_INPUTS + 3]
    begin, convolve, finish = back_compute(
        taps, refs[:BACK_INPUTS], made, small_made, rows, refs[BACK_INPUTS + 3 :], lambda group: None
    )
    begin()
    convolve(0, made.shape[1])
    finish()


def back(taps, operands):
    kernel, small, frames = operands[-1], operands[3], operands[0].shape[0]
    return pl.pallas_call(
        functools.partial(back_kernel, taps),
        out_shape=[
            jax.ShapeDtypeStruct(kernel.shape, jnp.bfloat16),
            jax.ShapeDtypeStruct(small.shape, jnp.bfloat16),
            jax.ShapeDtypeStruct((16, D), jnp.float32),
        ],
        in_specs=[VMEM] * (BACK_INPUTS - 1) + [HBM],
        out_specs=[VMEM] * 3,
        scratch_shapes=back_scratch(kernel.shape, frames),
        name="back",
        compiler_params=pltpu.CompilerParams(vmem_limit_bytes=48 * 1024 * 1024),
    )(*operands)


def back_reduce_kernel(sizes, shapes, taps, *refs):
    place = Place(*sizes)
    refs = list(refs)

    def pull(number):
        taken = refs[:number]
        del refs[:number]
        return taken

    count = len(KINDS)
    inputs, (block_grad,) = pull(BACK_INPUTS), pull(1)
    outs, (small_out, square_out, whole_box) = pull(count), pull(3)
    made, small_made, rows, scratch = *pull(3), pull(8)
    crossed, first_in, second_in, line_in = (pull(count) for _ in range(4))
    (held, group_box, dp_box, rows_low) = pull(4)
    sems = pull(11)
    (group_send, group_recv, dp_send, dp_recv, row_send, row_recv, pair_send, pair_recv) = pull(8)
    me = (place.dp, place.group)
    source = {"conv": made, "small": small_made, "blocks": block_grad}
    run = Reducer(
        place,
        shapes,
        None,
        (crossed, first_in, second_in, line_in, held, [source[kind] for kind in KINDS]),
        sems,
    )
    lines, b = run.lines, run.blocks
    conv, tiny = KINDS.index("conv"), KINDS.index("small")
    greet(place)

    def cross_all(k):
        for q in (1, 0):
            for p in (1, 0):

                def begin_one(index, _, p=p, q=q):
                    run.cross_of(k, p, q, run.turn(index)).start()
                    if k == b and q == 1:
                        run.load_of(p, q, run.turn(index)).start()
                    return 0

                lax.fori_loop(0, lines, begin_one, 0)

    def hook(group):
        pairs = shapes[conv][0]

        @pl.when(group % pairs == pairs - 1)
        def _():
            dp = group // pairs
            spot, flip_y = dp // 2, (dp % 2 + place.y) % 2
            for x in range(2):
                flip_x = (x + place.x) % 2
                p = flip_y * place.core + flip_x * (1 - place.core)
                q = flip_x * place.core + flip_y * (1 - place.core)
                run.cross_of(conv, p, q, spot).start()

    begin, convolve, finish = back_compute(taps, inputs, made, small_made, rows, scratch, hook)

    def remote(source, target, send, recv, device):
        return run.remote(source, target, send, recv, device)

    def each_other(size, mine, action):
        for other in range(size):
            pl.when(mine != other)(functools.partial(action, other))

    def group_copy(other):
        return remote(
            rows,
            group_box.at[place.group],
            group_send.at[other],
            group_recv.at[place.group],
            (place.dp, other),
        )

    def dp_copy(other):
        return remote(
            dp_box.at[place.dp], dp_box.at[place.dp], dp_send.at[other], dp_recv.at[place.dp], (other, place.group)
        )

    def group_wait(other):
        group_copy(other).wait_send()
        remote(rows, group_box.at[other], group_send.at[other], group_recv.at[other], me).wait_recv()

    def dp_wait(other):
        dp_copy(other).wait_send()
        remote(dp_box.at[other], dp_box.at[other], dp_send.at[other], dp_recv.at[other], me).wait_recv()

    def rows_to_group():
        group_box[place.group] = rows[...]
        each_other(place.group_size, place.group, lambda other: group_copy(other).start())

    def rows_to_all():
        each_other(place.group_size, place.group, group_wait)
        total = group_box[0]
        for other in range(1, place.group_size):
            total = total + group_box[other]
        dp_box[place.dp] = total
        each_other(place.dp_size, place.dp, lambda other: dp_copy(other).start())

    def some(first, last, action):
        def one(index, _):
            action(index)
            return 0

        lax.fori_loop(first, last, one, 0)

    members, depth = shapes[b][0], shapes[b][1]
    owners = Owners(place, members)
    my_rows = pl.ds(pl.multiple_of(place.dp * depth, depth), depth)
    owner_here = owners.here & (owners.group == place.group)
    owner_there = owners.here & (owners.group != place.group)

    def row_copy(member):
        return remote(
            rows_low.at[member],
            whole_box.at[my_rows],
            row_send.at[member],
            row_recv.at[place.dp],
            (owners.of(member), place.group),
        )

    def pair_copy(other):
        spot = pl.ds(pl.multiple_of(other * depth, depth), depth)
        return remote(
            whole_box.at[spot], whole_box.at[spot], pair_send.at[other], pair_recv.at[other], run.c_mate
        )

    def send_rows():
        rows_low[...] = outs[b][...].astype(jnp.bfloat16)
        for member in range(members):

            @pl.when(place.dp != owners.of(member))
            def _(member=member):
                row_copy(member).start()

            @pl.when(place.dp == owners.of(member))
            def _(member=member):
                whole_box[my_rows] = rows_low[member]
                pair_copy(place.dp).start()

    def take_rows():
        @pl.when(owner_here)
        def _():
            for other in range(place.dp_size):

                @pl.when(place.dp != other)
                def _(other=other):
                    spot = pl.ds(other * depth, depth)
                    remote(
                        rows_low.at[0], whole_box.at[spot], row_send.at[0], row_recv.at[other], me
                    ).wait_recv()
                    pair_copy(other).start()

        @pl.when(owner_there)
        def _():
            for other in range(place.dp_size):
                pair_copy(other).wait_recv()

    cross_all(b)
    begin()
    actions = {
        "one": lambda index, k: run.stage_one(k, index),
        "two": lambda index, k: run.stage_two(k, index),
        "edge": lambda index, k: run.line_step(k, index, False),
        "inner": lambda index, k: run.line_step(k, index, True),
        "end": lambda index, k: run.line_end(k, outs[k]),
    }

    def leave():
        finish()
        cross_all(tiny)
        rows_to_group()

    plain = {"leave": leave, "rows": send_rows, "take": take_rows}
    for name, kind, first, last in PLAN:
        if name == "groups":
            convolve(first, last)
        elif name in plain:
            plain[name]()
        else:
            action = functools.partial(lambda index, k, name: actions[name](index, k), k=KINDS.index(kind), name=name)
            if last - first == 1:
                action(first)
            else:
                some(first, last, action)
        if name == "rows":
            rows_to_all()
    square = jnp.sum(outs[b][...] * outs[b][...])
    for k in run.rest:
        square = square + jnp.sum(outs[k][...] * outs[k][...])
    each_other(place.dp_size, place.dp, dp_wait)
    total = dp_box[0]
    for other in range(1, place.dp_size):
        total = total + dp_box[other]
    small_out[...] = total
    skipped = lax.broadcasted_iota(jnp.int32, total.shape, 0) != LOSS_ROW
    square = square + jnp.sum(jnp.where(skipped, total * total, 0.0)) * (
        1.0 / (place.dp_size * place.group_size)
    )
    square_out[...] = jnp.full(square_out.shape, square, jnp.float32)
    for member in range(members):
        @pl.when(place.dp != owners.of(member))
        def _(member=member):
            row_copy(member).wait_send()

    @pl.when(owner_here)
    def _():
        for other in range(place.dp_size):
            pair_copy(other).wait_send()

    run.drain()


def back_reduce(sizes, shapes, taps, operands, block_grad):
    dp_size, group_size = sizes
    lines, count = dp_size // 2, len(KINDS)
    kernel, small, frames = operands[-1], operands[3], operands[0].shape[0]
    low, full = jnp.bfloat16, jnp.float32

    def boxes(lead):
        return [
            pltpu.VMEM(tuple(lead(kind)) + tuple(shape), low) for kind, shape in zip(KINDS, shapes)
        ]

    dma = pltpu.SemaphoreType.DMA
    scratch = (
        [pltpu.VMEM(kernel.shape, low), pltpu.VMEM(small.shape, low), pltpu.VMEM((16, D), full)]
        + back_scratch(kernel.shape, frames)
        + boxes(lambda kind: (2, 2, lines))
        + boxes(lambda kind: (2, lines))
        + boxes(lambda kind: (lines,))
        + boxes(lambda kind: (lines + 1,))
        + [
            pltpu.VMEM((2, lines) + tuple(shapes[-1]), low),
            pltpu.VMEM((group_size, 16, D), full),
            pltpu.VMEM((dp_size, 16, D), full),
            pltpu.VMEM(shapes[-1], low),
        ]
        + [dma((2, 2, lines))]
        + [dma((count, 2, 2, lines))] * 2
        + [dma((count, 2, lines))] * 2
        + [dma((count, lines))] * 6
        + [dma((group_size,))] * 2
        + [dma((dp_size,))] * 2
        + [dma((shapes[-1][0],)), dma((dp_size,))]
        + [dma((dp_size,))] * 2
    )
    return pl.pallas_call(
        functools.partial(back_reduce_kernel, sizes, shapes, taps),
        out_shape=[jax.ShapeDtypeStruct(shape, full) for shape in shapes]
        + [
            jax.ShapeDtypeStruct((16, D), full),
            jax.ShapeDtypeStruct((8, 128), full),
            jax.ShapeDtypeStruct((D, D), low),
        ],
        in_specs=[VMEM] * (BACK_INPUTS - 1) + [HBM, HBM],
        out_specs=[VMEM] * (count + 3),
        scratch_shapes=scratch,
        name="back_reduce",
        compiler_params=pltpu.CompilerParams(
            collective_id=1, has_side_effects=True, vmem_limit_bytes=VMEM_LIMIT
        ),
    )(*operands, block_grad)


PLAN = (
    ("one", "blocks", 0, 1),
    ("groups", "", 0, 3),
    ("one", "blocks", 4, 5),
    ("two", "blocks", 0, 1),
    ("groups", "", 3, 6),
    ("one", "blocks", 1, 2),
    ("groups", "", 6, 9),
    ("one", "blocks", 5, 6),
    ("two", "blocks", 1, 2),
    ("one", "blocks", 3, 4),
    ("groups", "", 9, 16),
    ("one", "blocks", 2, 3),
    ("leave", "", 0, 1),
    ("edge", "blocks", 0, 1),
    ("one", "blocks", 6, 7),
    ("one", "small", 1, 2),
    ("inner", "blocks", 2, 3),
    ("one", "blocks", 7, 8),
    ("one", "conv", 3, 4),
    ("two", "blocks", 2, 4),
    ("one", "conv", 0, 1),
    ("one", "small", 0, 1),
    ("one", "small", 5, 6),
    ("one", "small", 4, 5),
    ("one", "small", 2, 3),
    ("two", "small", 1, 2),
    ("edge", "blocks", 1, 2),
    ("inner", "blocks", 0, 1),
    ("one", "small", 3, 4),
    ("inner", "blocks", 1, 2),
    ("one", "conv", 5, 6),
    ("inner", "conv", 2, 3),
    ("one", "conv", 2, 3),
    ("edge", "blocks", 2, 3),
    ("two", "small", 0, 1),
    ("edge", "small", 0, 1),
    ("one", "conv", 1, 2),
    ("one", "conv", 4, 5),
    ("two", "small", 3, 4),
    ("end", "blocks", 0, 1),
    ("two", "conv", 0, 1),
    ("one", "small", 7, 8),
    ("inner", "small", 0, 1),
    ("two", "small", 2, 3),
    ("one", "conv", 7, 8),
    ("rows", "", 0, 1),
    ("inner", "small", 2, 3),
    ("one", "small", 6, 7),
    ("two", "conv", 1, 4),
    ("edge", "small", 1, 2),
    ("edge", "conv", 0, 1),
    ("inner", "small", 1, 2),
    ("one", "conv", 6, 7),
    ("edge", "conv", 1, 2),
    ("edge", "small", 2, 3),
    ("inner", "conv", 0, 1),
    ("edge", "conv", 2, 3),
    ("inner", "conv", 1, 2),
    ("take", "", 0, 1),
    ("end", "small", 0, 1),
    ("end", "conv", 0, 1),
)


GATHER_PLAN = (
    ("step", "small", 0),
    ("step", "conv", 0),
    ("step", "blocks", 0),
    ("enter", "", 0),
    ("step", "small", 1),
    ("step", "conv", 1),
    ("step", "blocks", 1),
    ("step", "conv", 2),
    ("step", "small", 2),
    ("step", "blocks", 2),
    ("step", "conv", 3),
    ("step", "small", 3),
    ("step", "conv", 4),
    ("step", "small", 4),
    ("step", "conv", 5),
    ("step", "small", 5),
    ("step", "small", 6),
    ("core", "conv", 0),
    ("core", "small", 0),
    ("compute", "", 0),
    ("step", "blocks", 3),
    ("compute", "", 1),
    ("compute", "", 2),
    ("compute", "", 3),
    ("step", "blocks", 4),
    ("step", "conv", 6),
    ("compute", "", 4),
    ("step", "blocks", 5),
    ("step", "blocks", 6),
)


def roots_kernel(sizes, members, *refs):
    (
        whole, stat, square_in, sides_out, update_out, square_out,
        gram, big, m0, m0b, m1, m1b, s1, s1b, s2b, s3, s3b, root, mixed,
        group_box, dp_box, group_send, group_recv, dp_send, dp_recv,
        side_send, side_recv, side_own, mixed_send, mixed_recv, update_send, update_recv, update_own,
    ) = refs
    place = Place(*sizes)
    owners = Owners(place, members)
    dp_size, rows = place.dp_size, D // place.dp_size
    me, c_mate = (place.dp, place.group), place.at(place.z, 0, 0, 1)
    owner = owners.here
    tile = 256
    greet(place)

    def remote(source, target, send, recv, device):
        return pltpu.make_async_remote_copy(
            src_ref=source,
            dst_ref=target,
            send_sem=send,
            recv_sem=recv,
            device_id=device,
            device_id_type=MESH,
        )

    def each_other(size, mine, action):
        for other in range(size):
            pl.when(mine != other)(functools.partial(action, other))

    def group_copy(other, slot):
        return remote(
            group_box.at[slot], group_box.at[slot], group_send.at[other], group_recv.at[slot], (place.dp, other)
        )

    def dp_copy(other, slot):
        return remote(dp_box.at[slot], dp_box.at[slot], dp_send.at[other], dp_recv.at[slot], (other, place.group))

    group_box[place.group] = square_in[...]
    each_other(place.group_size, place.group, lambda other: group_copy(other, place.group).start())

    def product_rows(one, two, then):
        def step(index, _):
            at = pl.ds(pl.multiple_of(index * tile, tile), tile)
            then(at, jnp.dot(one[at, :], two[...], preferred_element_type=jnp.float32))
            return 0

        lax.fori_loop(0, D // tile, step, 0)

    half = D // 2

    @pl.when(owner)
    def _():
        for index in range(2):
            at = slice(index * half, (index + 1) * half)

            @pl.when(place.core == 0)
            def _(at=at):
                gram[at, :] = dot_nt(whole[at, :], whole[...]).astype(jnp.bfloat16)

            @pl.when(place.core == 1)
            def _(at=at):
                gram[at, :] = dot_tn(whole[:, at], whole[...]).astype(jnp.bfloat16)

    def side_copy(other):
        spot = pl.ds(pl.multiple_of(other * rows, rows), rows)
        return remote(
            gram.at[spot],
            sides_out.at[owners.member, place.core],
            side_send.at[other],
            side_recv.at[owners.member, place.core],
            (other, owners.group),
        )

    def side_local():
        spot = pl.ds(pl.multiple_of(place.dp * rows, rows), rows)
        return pltpu.make_async_copy(gram.at[spot], sides_out.at[owners.member, place.core], side_own)

    def group_wait(other):
        group_copy(other, place.group).wait_send()
        group_copy(other, other).wait_recv()

    each_other(place.group_size, place.group, group_wait)
    total = group_box[0]
    for other in range(1, place.group_size):
        total = total + group_box[other]
    dp_box[place.dp] = total
    each_other(dp_size, place.dp, lambda other: dp_copy(other, place.dp).start())

    @pl.when(owner)
    def _():
        for other in range(dp_size):
            owners.to_rows(other, lambda other: side_copy(other).start(), lambda: side_local().start())

    def dp_wait(other):
        dp_copy(other, place.dp).wait_send()
        dp_copy(other, other).wait_recv()

    each_other(dp_size, place.dp, dp_wait)
    total = dp_box[0]
    for other in range(1, dp_size):
        total = total + dp_box[other]
    square_out[...] = total

    @pl.when(owner)
    def _():
        factor = jnp.minimum(1.0, max_norm / (jnp.sqrt(total[0:1, 0:1]) + 1e-06))
        square_factor = factor * factor
        spread_f = (1 - stat_decay) * square_factor

        def diagonal(at_start, shape):
            row = lax.broadcasted_iota(jnp.int32, shape, 0) + at_start
            return row == lax.broadcasted_iota(jnp.int32, shape, 1)

        def each_tile(action, carry):
            def step(index, carry):
                start = pl.multiple_of(index * tile, tile)
                return action(pl.ds(start, tile), start, carry)

            return lax.fori_loop(0, D // tile, step, carry)

        def renew(at, start, trace):
            value = stat_decay * stat[at, :].astype(jnp.float32) + spread_f * gram[at, :].astype(
                jnp.float32
            )
            big[at, :] = value
            on = jnp.where(diagonal(start, value.shape), value, 0.0)
            return trace + jnp.sum(jnp.sum(on, 1, keepdims=True), 0, keepdims=True)

        trace = each_tile(renew, jnp.zeros((1, 1), jnp.float32))
        damping = 0.0001 * (trace / D)

        def damp(at, start, total):
            value = big[at, :]
            value = value + jnp.where(diagonal(start, value.shape), damping, 0.0)
            big[at, :] = value
            return total + jnp.sum(jnp.sum(value * value, 1, keepdims=True), 0, keepdims=True)

        magnitude = jnp.sqrt(each_tile(damp, jnp.zeros((1, 1), jnp.float32)))

        def scale(at, start, carry):
            value = big[at, :] / magnitude
            m0[at, :] = value
            m0b[at, :] = value.astype(jnp.bfloat16)
            return carry

        each_tile(scale, 0)
        a = 1.5625

        def square_of(source):
            def then(at, value):
                value = value * 0.0625 - 0.625 * source[at, :]
                s1[at, :] = value
                s1b[at, :] = value.astype(jnp.bfloat16)

            return then

        def fourth(at, value):
            s2b[at, :] = (value + (2 * a) * s1[at, :]).astype(jnp.bfloat16)

        product_rows(m0b, m0b, square_of(m0))
        product_rows(s1b, s1b, fourth)

        def next_one(at, value):
            value = value + (a * a) * m0[at, :]
            m1[at, :] = value
            m1b[at, :] = value.astype(jnp.bfloat16)

        product_rows(s2b, m0b, next_one)

        def joined(at, value):
            value = value * 0.0625 - 0.3125 * (m0[at, :] + m1[at, :])
            s3[at, :] = value
            s3b[at, :] = value.astype(jnp.bfloat16)

        product_rows(m0b, m1b, joined)
        product_rows(m1b, m1b, square_of(m1))
        product_rows(s1b, s1b, fourth)

        def next_two(at, value):
            value = value + (a * a) * m1[at, :]
            m0[at, :] = value
            m0b[at, :] = value.astype(jnp.bfloat16)

        product_rows(s2b, m1b, next_two)
        outer = lax.rsqrt(jnp.sqrt(magnitude))

        def final(at, value):
            value = 1.25 * s3[at, :] - (0.25 * a) * m0[at, :] - 0.25 * value
            start = at.start
            value = value + jnp.where(diagonal(start, value.shape), 1.25 * a, 0.0)
            root[at, :] = (value * outer).astype(jnp.bfloat16)

        product_rows(s3b, m0b, final)

    per_part = dp_size // 2

    def mixed_copy(part):
        at = pl.ds(part * half, half)
        return remote(mixed.at[at], mixed.at[at], mixed_send.at[part], mixed_recv.at[part], c_mate)

    def update_copy(other):
        spot = pl.ds(pl.multiple_of(other * rows, rows), rows)
        return remote(
            m1b.at[spot],
            update_out.at[owners.member],
            update_send.at[other],
            update_recv.at[owners.member],
            (other, owners.group),
        )

    def update_local():
        spot = pl.ds(pl.multiple_of(place.dp * rows, rows), rows)
        return pltpu.make_async_copy(m1b.at[spot], update_out.at[owners.member], update_own)

    @pl.when(owner & (place.core == 0))
    def _():
        for part in range(2):
            at = slice(part * half, (part + 1) * half)
            mixed[at, :] = dot(root[at, :], whole[...]).astype(jnp.bfloat16)
            mixed_copy(part).start()
        for part in range(2):
            mixed_copy(part).wait_send()

    @pl.when(owner & (place.core == 1))
    def _():
        for part in range(2):
            mixed_copy(part).wait_recv()
            at = slice(part * half, (part + 1) * half)
            m1b[at, :] = dot(mixed[at, :], root[...]).astype(jnp.bfloat16)
            for other in range(part * per_part, (part + 1) * per_part):
                owners.to_rows(
                    other, lambda other: update_copy(other).start(), lambda: update_local().start()
                )
        for other in range(dp_size):
            owners.to_rows(
                other, lambda other: update_copy(other).wait_send(), lambda: update_local().wait()
            )

    @pl.when(owner)
    def _():
        for other in range(dp_size):
            owners.to_rows(
                other, lambda other: side_copy(other).wait_send(), lambda: side_local().wait()
            )

    for member in range(members):
        for side in range(2):

            @pl.when((place.dp != owners.of(member)) | (place.core != side))
            def _(member=member, side=side):
                remote(
                    gram.at[pl.ds(0, rows)],
                    sides_out.at[member, side],
                    side_send.at[0],
                    side_recv.at[member, side],
                    me,
                ).wait_recv()

        @pl.when((place.dp != owners.of(member)) | (place.core != 1))
        def _(member=member):
            remote(
                m1b.at[pl.ds(0, rows)],
                update_out.at[member],
                update_send.at[0],
                update_recv.at[member],
                me,
            ).wait_recv()


def shampoo_roots(sizes, members, whole, stat, square):
    dp_size, group_size = sizes
    rows = D // dp_size
    low, full = jnp.bfloat16, jnp.float32
    dma = pltpu.SemaphoreType.DMA
    half, word = pltpu.VMEM((D, D), low), pltpu.VMEM((D, D), full)
    return pl.pallas_call(
        functools.partial(roots_kernel, sizes, members),
        out_shape=[
            jax.ShapeDtypeStruct((members, 2, rows, D), low),
            jax.ShapeDtypeStruct((members, rows, D), low),
            jax.ShapeDtypeStruct((8, 128), full),
        ],
        in_specs=[VMEM] * 3,
        out_specs=[VMEM] * 3,
        scratch_shapes=[half, word, word, half, word, half, word, half, half, word, half, half, half]
        + [pltpu.VMEM((group_size, 8, 128), full), pltpu.VMEM((dp_size, 8, 128), full)]
        + [dma((group_size,))] * 2
        + [dma((dp_size,))] * 2
        + [dma((dp_size,)), dma((members, 2)), dma]
        + [dma((2,)), dma((2,))]
        + [dma((dp_size,)), dma((members,)), dma],
        name="shampoo_roots",
        compiler_params=pltpu.CompilerParams(
            collective_id=2, has_side_effects=True, vmem_limit_bytes=VMEM_LIMIT
        ),
    )(whole, stat, square)


def finish_kernel(rates, *refs):
    square, rows, block_sum, small, kernel, sides, update = refs[:7]
    weights, blocks, statistics = refs[7:25], refs[25], refs[26]
    norm_out, outs = refs[27], refs[28:46]
    block_out, stat_out, blocks_out, loss_out = refs[46:]
    loss_out[...] = rows[LOSS_ROW : LOSS_ROW + 1, 0:1]
    norm = jnp.sqrt(square[0:1, 0:1])
    norm_out[...] = norm
    factor = jnp.minimum(1.0, max_norm / (norm + 1e-06))

    def renew(index, at, grad):
        rate, decay = rates[index]
        ins, out = weights[3 * index : 3 * index + 3], outs[3 * index : 3 * index + 3]
        result = adamw(ins[0][at], grad * factor, ins[1][at], ins[2][at], rate, decay)
        for ref, value in zip(out, result):
            ref[at] = value

    width = weights[0].shape[1]
    vector_rows = weights[6].shape[0]
    renew(0, ..., rows[LOSS_ROW + 1 : LOSS_ROW + 3, :width])
    renew(1, (slice(None), slice(0, 128)), small[0:64, :])
    renew(1, (slice(None), slice(128, 192)), small[64:128, 0:64])
    renew(2, ..., rows[0:vector_rows, :])
    runs, steps, c, channels = weights[9].shape
    for offset in range(steps):
        parts = [kernel[group, offset * c : (offset + 1) * c, :] for group in range(channels // c)]
        renew(
            3,
            (slice(None), offset),
            jnp.concatenate(parts, 0).T.reshape(runs, c, channels),
        )
    renew(4, ..., small[128:224, :].T[0:64])
    renew(5, ..., small[224:256, 0:CLUSTER_ROWS])
    for member in range(blocks.shape[0]):
        block_out[member] = block_sum[member] * factor
        step = update[member].astype(jnp.float32) * factor + decay_weight * blocks[member]
        blocks_out[member] = blocks[member] - rate_shampoo * step
        for side in range(2):
            spread = (1 - stat_decay) * factor * factor
            stat_out[member, side] = stat_decay * statistics[member, side] + spread * sides[
                member, side
            ].astype(jnp.float32)


def finish(sums, weights, blocks, statistics):
    full = jnp.float32
    rates = [(rate_vector, 0.0), (rate_matrix, decay_weight), (rate_vector, 0.0)]
    rates += [(rate_matrix, decay_weight)] * 3
    operands = [*sums, *weights, blocks, statistics]
    shapes = [(1, 1)] + [weight.shape for weight in weights]
    shapes += [blocks.shape, statistics.shape, blocks.shape, (1, 1)]
    return pl.pallas_call(
        functools.partial(finish_kernel, rates),
        out_shape=[jax.ShapeDtypeStruct(shape, full) for shape in shapes],
        in_specs=[VMEM] * len(operands),
        out_specs=[VMEM] * len(shapes),
        name="finish",
        compiler_params=pltpu.CompilerParams(vmem_limit_bytes=VMEM_LIMIT),
    )(*operands)


def conv_to_shard(weight):
    taps, c, channels = weight.shape
    split = weight.reshape(taps // STRIDE, STRIDE, c, channels // c, c)
    return split.transpose(3, 1, 4, 0, 2).reshape(channels // c, STRIDE * c, taps // STRIDE * c)


def conv_from_shard(shard):
    groups, rows, columns = shard.shape
    c = rows // STRIDE
    split = shard.reshape(groups, STRIDE, c, columns // c, c)
    return split.transpose(3, 1, 4, 0, 2).reshape(columns // c * STRIDE, c, groups * c)


def pack_small(projection, head, clusters, note):
    lead, kind = projection.shape[:-2], projection.dtype
    notes = jnp.broadcast_to(note, lead + (32, 2)).astype(kind)
    return jnp.concatenate(
        [
            projection[..., :128],
            jnp.concatenate([projection[..., 128:], jnp.zeros(lead + (64, 64), kind)], -1),
            jnp.concatenate([head, jnp.zeros(lead + (96, 64), kind)], -1),
            jnp.concatenate([jnp.swapaxes(clusters, -1, -2), notes], -1),
        ],
        -2,
    )


def unpack_small(packed):
    projection = jnp.concatenate([packed[..., :64, :], packed[..., 64:128, :64]], -1)
    head = packed[..., 128:224, :64]
    clusters = jnp.swapaxes(packed[..., 224:, :CLUSTER_ROWS], -1, -2)
    return projection, head, clusters


def pack_whole(projection, head, clusters, note):
    def cut(values, down, across):
        rows, columns = values.shape
        return values.reshape(down, rows // down, across, columns // across).transpose(0, 2, 1, 3)

    return pack_small(
        cut(projection, 8, 4), cut(head, 8, 4), cut(clusters, 4, 8).transpose(1, 0, 2, 3), note
    )


def unpack_whole(packed):
    def join(values):
        down, across, rows, columns = values.shape
        return values.transpose(0, 2, 1, 3).reshape(down * rows, across * columns)

    projection, head, clusters = unpack_small(packed)
    return join(projection), join(head), join(clusters.transpose(1, 0, 2, 3))


def parts_of_rows(rows, vector_rows, width):
    return rows[:vector_rows], rows[vector_rows + 1 : vector_rows + 3, :width], rows[vector_rows, 0]


CLUSTER_ROWS = 126
SMALL = ((64, 192), (96, 64), (CLUSTER_ROWS, 32))


def body(
    sizes,
    features,
    span_starts,
    labels,
    feature_norm,
    feature_first,
    feature_second,
    projection,
    projection_first,
    projection_second,
    vectors,
    vector_first,
    vector_second,
    conv_weight,
    conv_first,
    conv_second,
    head,
    head_first,
    head_second,
    clusters,
    cluster_first,
    cluster_second,
    blocks,
    statistics,
):
    dp_size, group_size = sizes
    members, rows = blocks.shape[0], blocks.shape[1]
    masks = jax.vmap(jax.vmap(frame_mask))(span_starts)
    local_count = jnp.sum(masks)
    fast = (
        rows % 16 == 0
        and dp_size % 2 == 0
        and group_size == 4
        and dp_size >= 2 * members
        and (projection.shape, head.shape, clusters.shape) == SMALL
        and conv_weight.shape[2] % conv_weight.shape[1] == 0
        and masks.size <= 256
    )
    frames, vector_rows, width = masks.size, vectors.shape[0], feature_norm.shape[1]
    flat = features.reshape(frames, -1)

    def runs(values):
        return values.reshape((-1, STRIDE) + values.shape[1:])

    if fast:
        taps, c, channels = conv_weight.shape
        taps *= group_size
        shapes = [
            (channels // c, STRIDE * c, taps // group_size // STRIDE * c),
            (256, 128),
            blocks.shape,
        ]
        raw = (
            span_starts.reshape(-1, span_starts.shape[-1]),
            projection, runs(conv_weight), head.T, clusters.T, blocks, statistics,
        )
        kernel_w, small_w, blocks_w, *saved, mask, stats_low = gather_weights(
            sizes, shapes, taps, raw, flat, feature_norm, vectors
        )
    else:
        proj_w, kernel_full, head_w, clusters_w, blocks_w = gather_plain(
            projection, conv_weight, head, clusters, blocks
        )
        whole = conv_to_shard(kernel_full)
        kernel_w = whole.reshape(whole.shape[:2] + (4, -1)).transpose(2, 0, 1, 3)
        count = lax.psum(local_count, ("dp", "group"))
        high = jnp.floor(count / 256.0) * 256.0
        notes = jnp.concatenate([jnp.stack([high, count - high]), jnp.zeros(30, jnp.float32)])
        small_w = pack_whole(proj_w, head_w, clusters_w, notes.reshape(8, 4, 1, 1))
        taps = kernel_w.shape[0] * kernel_w.shape[3] // (D // kernel_w.shape[1]) * STRIDE
        mask = masks.reshape(frames, 1)
        saved = front(flat, mask, feature_norm, vectors, small_w, kernel_w, taps)
    feature_unit, normed, hidden_t, encoded, encoder_unit, encoder_inverse, slope = saved
    extra_parts = (sizes, stats_low) if fast else ()
    encoded_grad, block_part, head_part, center_part, trunk_rows, counted, *stat_whole = trunk(
        encoded, mask, labels.reshape(frames, 1), vectors, small_w, blocks_w, *extra_parts
    )
    masked_count = counted[0, 0]
    operands = (
        encoded_grad, mask, vectors, small_w, feature_unit, normed, hidden_t,
        encoder_unit, encoder_inverse, slope, trunk_rows, head_part, center_part, kernel_w,
    )
    if fast:
        kernel_sum, small_sum, block_sum, extra, square, whole = back_reduce(
            sizes, shapes, taps, operands, block_part
        )
        sides, update_rows, square = shampoo_roots(sizes, members, whole, *stat_whole, square)

        done = finish(
            (square, extra, block_sum, small_sum, kernel_sum, sides, update_rows),
            (
                feature_norm, feature_first, feature_second,
                projection, projection_first, projection_second,
                vectors, vector_first, vector_second,
                runs(conv_weight), runs(conv_first), runs(conv_second),
                head.T, head_first.T, head_second.T,
                clusters.T, cluster_first.T, cluster_second.T,
            ),
            blocks,
            statistics,
        )
        outs = []
        for index in range(0, 18, 3):
            parts = done[1 + index : 4 + index]
            if index == 9:
                parts = [part.reshape(conv_weight.shape) for part in parts]
            if index >= 12:
                parts = [part.T for part in parts]
            outs += parts
        return (done[-1][0, 0], masked_count, done[0][0, 0], *outs, *done[19:22])
    kernel_part, small_part, row_part = back(taps, operands)
    proj_part, head_part, center_part = unpack_whole(small_part)
    kernel_plain = conv_from_shard(
        kernel_part.transpose(1, 2, 0, 3).reshape(kernel_part.shape[1:3] + (-1,))
    )
    large_total = reduce_grads(
        tuple(
            part.astype(jnp.float32)
            for part in (proj_part, kernel_plain, head_part, center_part, block_part)
        )
    )
    vector_grad, feature_grad, loss_sum = parts_of_rows(
        lax.psum(row_part, ("dp", "group")), vector_rows, width
    )
    local_squares = sum((jnp.sum(part * part) for part in large_total))
    norm_square = (
        lax.psum(local_squares, ("dp", "group"))
        + jnp.sum(feature_grad * feature_grad)
        + jnp.sum(vector_grad * vector_grad)
    )
    grad_norm = jnp.sqrt(norm_square)
    factor = jnp.minimum(1.0, max_norm / (grad_norm + 1e-06))
    proj_grad, kernel_grad, head_grad, cluster_grad, block_rows = [
        part * factor for part in large_total
    ]
    feature_out = adamw(
        feature_norm, feature_grad * factor, feature_first, feature_second, rate_vector, 0.0
    )
    projection_out = adamw(
        projection, proj_grad, projection_first, projection_second, rate_matrix, decay_weight
    )
    vector_out = adamw(vectors, vector_grad * factor, vector_first, vector_second, rate_vector, 0.0)
    conv_out = adamw(conv_weight, kernel_grad, conv_first, conv_second, rate_matrix, decay_weight)
    head_out = adamw(head, head_grad, head_first, head_second, rate_matrix, decay_weight)
    cluster_out = adamw(
        clusters, cluster_grad, cluster_first, cluster_second, rate_matrix, decay_weight
    )
    statistics_new, update_rows = shampoo_plain(block_rows, statistics)
    blocks_new = blocks - rate_shampoo * (update_rows + decay_weight * blocks)
    return (
        loss_sum,
        masked_count,
        grad_norm,
        *feature_out,
        *projection_out,
        *vector_out,
        *conv_out,
        *head_out,
        *cluster_out,
        block_rows,
        statistics_new,
        blocks_new,
    )


def solution(mesh):
    in_specs = (
        P(None, ("dp", "group"), None, None),
        P(None, ("dp", "group"), None),
        P(None, ("dp", "group"), None),
        P(),
        P(),
        P(),
        P("dp", "group"),
        P("dp", "group"),
        P("dp", "group"),
        P(),
        P(),
        P(),
        P("group", None, "dp"),
        P("group", None, "dp"),
        P("group", None, "dp"),
        P("dp", "group"),
        P("dp", "group"),
        P("dp", "group"),
        P("group", "dp"),
        P("group", "dp"),
        P("group", "dp"),
        P("group", "dp", None),
        P("group", None, "dp", None),
    )
    out_specs = (
        P(),
        P(),
        P(),
        P(),
        P(),
        P(),
        P("dp", "group"),
        P("dp", "group"),
        P("dp", "group"),
        P(),
        P(),
        P(),
        P("group", None, "dp"),
        P("group", None, "dp"),
        P("group", None, "dp"),
        P("dp", "group"),
        P("dp", "group"),
        P("dp", "group"),
        P("group", "dp"),
        P("group", "dp"),
        P("group", "dp"),
        P("group", "dp", None),
        P("group", None, "dp", None),
        P("group", "dp", None),
    )
    return jax.shard_map(
        functools.partial(body, (mesh.shape["dp"], mesh.shape["group"])), mesh=mesh, in_specs=in_specs, out_specs=out_specs, check_vma=False)
```

profile of v0, /device:TPU:13, one launch (start us, length us, event | category | flops | bytes accessed | tf_op | source)
XLA Modules:
  0.0 361.3 jit_solution(7594584042547859318)
XLA Ops:
  0.7 1.5 copy.47.refs_2_
  2.1 110.0 %gather_front.1 = (bf16[4,16,192,384]{3,2,1,0:T(8,128)(2,1)}, bf16[8,4,256,128]{3,2,1,0:T(8,128)(2,1)}, bf16[12,768,768]{2,1,0:T(8,128)(2,1)}, f32[256,512]{1,0:...) custom-call(s32[2,10]{1,0:T(2,128)} %bitcast.38, ...), custom_call_target="tpu_custom_call" | custom-call | tf_op jit(solution)/shard_map/gather_front/pallas_call | solution.py:449
  112.2 39.9 %trunk.1 = (f32[256,768]{1,0:T(8,128)}, bf16[12,768,768]{2,1,0:T(8,128)(2,1)}, bf16[768,512]{1,0:T(8,128)(2,1)}, f32[256,512]{1,0:T(8,128)}, f32[8,768]{1,0:T(8,...) custom-call(f32[256,768]{1,0:T(8,128)} %get-tuple-element.75.refs_0_, f32[256,1]{1,0:T(8,128)} %get-tuple-element.76.refs_1_, ...), custom_call_target="tpu_custom_call" | custom-call | tf_op jit(solution)/shard_map/trunk/pallas_call | solution.py:997
  152.1 145.7 %back_reduce.1 = (f32[2,192,384]{2,1,0:T(8,128)}, f32[256,128]{1,0:T(8,128)}, f32[3,96,768]{2,1,0:T(8,128)}, f32[16,768]{1,0:T(8,128)}, f32[8,128]{1,0:T(8,128)}, /*index=5*/bf16[768,768]{1,0:T(8,128)(2,1)}) custom-call(f32[256,768]{1,0:T(8,128)} %get-tuple-element.80.refs_0_, f32[256,1]{1,0:T(8,128)} %get-tuple-element.76.refs_1_, f32[7,768]{1,0:T(8,128)} %refs_13_.1, ...), custom_call_target="tpu_custom_call" | custom-call | tf_op jit(solution)/shard_map/back_reduce/pallas_call | solution.py:1640
  297.8 54.3 %shampoo_roots.1 = (bf16[3,2,96,768]{3,2,1,0:T(8,128)(2,1)}, bf16[3,96,768]{2,1,0:T(8,128)(2,1)}, f32[8,128]{1,0:T(8,128)}) custom-call(bf16[768,768]{1,0:T(8,128)(2,1)} %get-tuple-element.92.refs_0_, bf16[768,768]{1,0:T(8,128)(2,1)} %get-tuple-element.93.refs_1_, f32[8,128]{1,0:T(8,128)} %get-tuple-element.94.refs_2_), custom_call_target="tpu_custom_call" | custom-call | tf_op jit(solution)/shard_map/shampoo_roots/pallas_call | solution.py:2031
  352.1 7.1 %finish.1 = (f32[1,1]{1,0:T(1,128)}, f32[2,512]{1,0:T(2,128)}, f32[2,512]{1,0:T(2,128)}, f32[2,512]{1,0:T(2,128)}, f32[64,192]{1,0:T(8,128)}, /*index=5*/f32[64,...) custom-call(f32[8,128]{1,0:T(8,128)} %get-tuple-element.95.refs_0_, ...), custom_call_target="tpu_custom_call" | custom-call | tf_op jit(solution)/shard_map/finish/pallas_call | solution.py:2105
where the time goes:
time: 366 us; the launch traced here: 361 us
  Pallas kernels  357 us (98%)
    pallas_call x1, Pallas kernels, back_reduce(): pl.pallas_call(functools.partial(back_reduce_kernel, sizes, shapes, taps)...  146 us
    pallas_call x1, Pallas kernels, gather_weights(): pl.pallas_call(functools.partial(gather_kernel, sizes, shapes, taps), out...  110 us
    pallas_call x1, Pallas kernels, shampoo_roots(): pl.pallas_call(functools.partial(roots_kernel, sizes, members), out_shape...  54.3 us
    pallas_call x1, Pallas kernels, trunk(): pl.pallas_call(functools.partial(trunk_kernel, sizes), out_shape=[out((fr...  39.9 us

commit v1 on v0

--- a/solution.py
+++ b/solution.py
@@ -241,8 +241,8 @@
 KINDS = ("conv", "small", "blocks")
 
 
-def make_shards(refs, mask, conv, small, blocks_low, stats_low):
-    starts, projection, weight, head_t, clusters_t, blocks, statistics = refs
+def make_shards(refs, mask, conv, small):
+    starts, projection, weight, head_t, clusters_t = refs
     for clip in range(starts.shape[0]):
         frame = lax.broadcasted_iota(jnp.int32, (CLIP, starts.shape[1]), 0)
         begins = starts[clip : clip + 1, :]
@@ -265,8 +265,6 @@
     small[128:224, :] = padded(head_t[...].T).astype(low)
     lane = lax.broadcasted_iota(jnp.int32, (32, 128), 1)
     small[224:256, :] = jnp.where(lane < CLUSTER_ROWS, padded(clusters_t[...]), note).astype(low)
-    blocks_low[...] = blocks[...].astype(low)
-    stats_low[...] = statistics[...].astype(low)
 
 
 def gather_kernel(sizes, shapes, taps, *refs):
@@ -285,7 +283,7 @@
     (send_sem, recv_sem, own_sem, small_sem) = pull(4)
     z, last = place.z, place.lines - 1
     me = (place.dp, place.group)
-    make_shards(raw, mask, *ins, stats_low)
+    make_shards(raw[:5], mask, *ins[:2])
     greet(place)
     sent = []
     slots = [0] * count
@@ -409,6 +407,8 @@
     for name, kind, step in GATHER_PLAN:
         if name == "step":
             k = KINDS.index(kind)
+            if step == 0 and kind == "blocks":
+                ins[k][...] = raw[5][...].astype(jnp.bfloat16)
             (step_z_second if kind == "blocks" else step_z_first)(k, step)
             if step == 0:
                 own_copies[k].start()
@@ -417,6 +417,7 @@
             own_copies[KINDS.index(kind)].wait()
         elif name == "enter":
             enter()
+            stats_low[...] = raw[6][...].astype(jnp.bfloat16)
         else:
             compute(step)
     from_core(KINDS.index("blocks"))
@@ -600,7 +601,7 @@
         action(pl.ds(pl.multiple_of(index * tile, tile), tile))
         return 0
 
-    lax.fori_loop(0, total // tile, step, 0, unroll=2)
+    lax.fori_loop(0, total // tile, step, 0, unroll=4)
 
 
 def dot(one, two):
@@ -1799,7 +1800,7 @@
             then(at, jnp.dot(one[at, :], two[...], preferred_element_type=jnp.float32))
             return 0
 
-        lax.fori_loop(0, D // tile, step, 0)
+        lax.fori_loop(0, D // tile, step, 0, unroll=True)
 
     half = D // 2
 
@@ -1871,7 +1872,7 @@
                 start = pl.multiple_of(index * tile, tile)
                 return action(pl.ds(start, tile), start, carry)
 
-            return lax.fori_loop(0, D // tile, step, carry)
+            return lax.fori_loop(0, D // tile, step, carry, unroll=True)
 
         def renew(at, start, trace):
             value = stat_decay * stat[at, :].astype(jnp.float32) + spread_f * gram[at, :].astype(

time: 366 us -> 365 us (level)
  no operation moved by 1% of the time
where the time goes in v1:
time: 365 us; the launch traced here: 361 us
  Pallas kernels  356 us (98%)
    pallas_call x1, Pallas kernels, back_reduce(): pl.pallas_call(functools.partial(back_reduce_kernel, sizes, shapes, taps)...  146 us
    pallas_call x1, Pallas kernels, gather_weights(): pl.pallas_call(functools.partial(gather_kernel, sizes, shapes, taps), out...  110 us
    pallas_call x1, Pallas kernels, shampoo_roots(): pl.pallas_call(functools.partial(roots_kernel, sizes, members), out_shape...  54 us
    pallas_call x1, Pallas kernels, trunk(): pl.pallas_call(functools.partial(trunk_kernel, sizes), out_shape=[out((fr...  39 us

profile of v1, /device:TPU:13, one launch (start us, length us, event | category | flops | bytes accessed | tf_op | source)
XLA Modules:
  0.0 360.5 jit_solution(12005572348540892507)
XLA Ops:
  0.7 1.5 copy.47.refs_2_
  2.1 109.9 %gather_front.1 = (bf16[4,16,192,384]{3,2,1,0:T(8,128)(2,1)}, bf16[8,4,256,128]{3,2,1,0:T(8,128)(2,1)}, bf16[12,768,768]{2,1,0:T(8,128)(2,1)}, f32[256,512]{1,0:...) custom-call(s32[2,10]{1,0:T(2,128)} %bitcast.38, ...), custom_call_target="tpu_custom_call" | custom-call | tf_op jit(solution)/shard_map/gather_front/pallas_call | solution.py:450
  112.1 39.0 %trunk.1 = (f32[256,768]{1,0:T(8,128)}, bf16[12,768,768]{2,1,0:T(8,128)(2,1)}, bf16[768,512]{1,0:T(8,128)(2,1)}, f32[256,512]{1,0:T(8,128)}, f32[8,768]{1,0:T(8,...) custom-call(f32[256,768]{1,0:T(8,128)} %get-tuple-element.75.refs_0_, f32[256,1]{1,0:T(8,128)} %get-tuple-element.76.refs_1_, ...), custom_call_target="tpu_custom_call" | custom-call | tf_op jit(solution)/shard_map/trunk/pallas_call | solution.py:998
  151.1 146.3 %back_reduce.1 = (f32[2,192,384]{2,1,0:T(8,128)}, f32[256,128]{1,0:T(8,128)}, f32[3,96,768]{2,1,0:T(8,128)}, f32[16,768]{1,0:T(8,128)}, f32[8,128]{1,0:T(8,128)}, /*index=5*/bf16[768,768]{1,0:T(8,128)(2,1)}) custom-call(f32[256,768]{1,0:T(8,128)} %get-tuple-element.80.refs_0_, f32[256,1]{1,0:T(8,128)} %get-tuple-element.76.refs_1_, f32[7,768]{1,0:T(8,128)} %refs_13_.1, ...), custom_call_target="tpu_custom_call" | custom-call | tf_op jit(solution)/shard_map/back_reduce/pallas_call | solution.py:1641
  297.4 54.0 %shampoo_roots.1 = (bf16[3,2,96,768]{3,2,1,0:T(8,128)(2,1)}, bf16[3,96,768]{2,1,0:T(8,128)(2,1)}, f32[8,128]{1,0:T(8,128)}) custom-call(bf16[768,768]{1,0:T(8,128)(2,1)} %get-tuple-element.92.refs_0_, bf16[768,768]{1,0:T(8,128)(2,1)} %get-tuple-element.93.refs_1_, f32[8,128]{1,0:T(8,128)} %get-tuple-element.94.refs_2_), custom_call_target="tpu_custom_call" | custom-call | tf_op jit(solution)/shard_map/shampoo_roots/pallas_call | solution.py:2032
  351.4 7.1 %finish.1 = (f32[1,1]{1,0:T(1,128)}, f32[2,512]{1,0:T(2,128)}, f32[2,512]{1,0:T(2,128)}, f32[2,512]{1,0:T(2,128)}, f32[64,192]{1,0:T(8,128)}, /*index=5*/f32[64,...) custom-call(f32[8,128]{1,0:T(8,128)} %get-tuple-element.95.refs_0_, ...), custom_call_target="tpu_custom_call" | custom-call | tf_op jit(solution)/shard_map/finish/pallas_call | solution.py:2106
